TPU v7x, 256 devices: a whole 4x4x8 slice. The times are simulated.
256 devices in a mesh: dp: 32 (over x, z_hi, core), tensor: 8 (over z_lo, y).
Axes of the slice: x: 4, y: 4, z: 8 (z_hi: 4, z_lo: 2; z = z_hi * 2 + z_lo), core: 2. Of those that a mesh axis runs over, the one named last changes fastest.
Arguments:
- acts: bfloat16 [8192, 4096], P('dp', 'tensor'), may hold values from -6 to 6
- cotangent: bfloat16 [8192, 5120], P('dp', 'tensor'), may hold values from -6 to 6
- out_weight: bfloat16 [4096, 5120], P('tensor'), may hold values from -0.09375 to 0.09375
- old_a: bfloat16 [32, 128, 64], P('tensor'), may hold values from -0.09375 to 0.09375
- old_b: bfloat16 [64, 5120], replicated, may hold values from -0.75 to 0.75
- master_a: float32 [32, 128, 64], P('tensor', 'dp'), may hold values from -0.09375 to 0.09375
- master_b: float32 [64, 5120], P('dp', 'tensor'), may hold values from -0.75 to 0.75
- moment_a: float32 [32, 128, 64], P('tensor', 'dp'), may hold values from -0.15625 to 0.15625
- moment_b: float32 [64, 5120], P('dp', 'tensor'), may hold values from -0.15625 to 0.15625
- second_a: float32 [32, 128, 64], P('tensor', 'dp'), may hold values from 0.0001 to 0.01
- second_b: float32 [64, 5120], P('dp', 'tensor'), may hold values from 0.0001 to 0.01
- key_cache: bfloat16 [4096, 8, 48, 128], P('dp', 'tensor'), may hold values from -6 to 6
- value_cache: bfloat16 [4096, 8, 48, 128], P('dp', 'tensor'), may hold values from -6 to 6
- lengths: int32 [4096], P('dp'), may hold values from 1 to 48, as said below
- new_query: bfloat16 [4096, 3, 4096], P('dp', None, 'tensor'), may hold values from -100 to 100
- new_key: bfloat16 [4096, 3, 1024], P('dp', None, 'tensor'), may hold values from -8 to 8
- new_value: bfloat16 [4096, 3, 1024], P('dp', None, 'tensor'), may hold values from -6 to 6
Outputs:
- attention_output_gradient: bfloat16 [8192, 4096], P('dp', 'tensor')
- new_master_a: float32 [32, 128, 64], P('tensor', 'dp')
- new_master_b: float32 [64, 5120], P('dp', 'tensor')
- new_moment_a: float32 [32, 128, 64], P('tensor', 'dp')
- new_moment_b: float32 [64, 5120], P('dp', 'tensor')
- new_second_a: float32 [32, 128, 64], P('tensor', 'dp')
- new_second_b: float32 [64, 5120], P('dp', 'tensor')
- decoded_projection_output: bfloat16 [5120, 12288], P('tensor', 'dp')
Inputs may be any that keep to these rules, and one draw needn't show every extreme that they name: `lengths`: every rollout group has a row that fills all 48 slots.
All inputs are finite; a program needn't handle non-finite values.
Results may differ from a plain program's by a relative error of at most 0.0067.
Values may be sent and summed in bfloat16 or wider, within the bound.
A program may use at most 128 MiB of HBM per device.

v0:
```python
import jax
import jax.numpy as jnp
from jax import lax
from jax.sharding import PartitionSpec as P

adapter_scale = 2.0
beta_one = 0.9
beta_two = 0.999
learn_rate = 0.01
decay_rate = 0.01
corr_one = 1.0 - 0.9**10
corr_two = 1.0 - 0.999**10


def adam_step(master, moment, second, grad):
    moment_new = beta_one * moment + (1.0 - beta_one) * grad
    second_new = beta_two * second + (1.0 - beta_two) * grad * grad
    update = moment_new / corr_one / (jnp.sqrt(second_new / corr_two) + 1e-08)
    return (master - learn_rate * (update + decay_rate * master), moment_new, second_new)


def attend_block(query, keys, values, lengths, new_key, new_value):
    rows = query.shape[0]
    steps = query.shape[1]
    kv_heads = keys.shape[1]
    head_size = keys.shape[3]
    slots = keys.shape[2]
    group = query.shape[2] // (kv_heads * head_size)
    qb = query.reshape(rows, steps, kv_heads, group, head_size)
    knew = new_key.reshape(rows, steps, kv_heads, head_size)
    vnew = new_value.reshape(rows, steps, kv_heads, head_size)
    adapter_factor = 1.0 / jnp.sqrt(jnp.float32(head_size))
    cache_scores = (
        jnp.einsum("bsngd,bncd->bsngc", qb, keys, preferred_element_type=jnp.float32)
        * adapter_factor
    )
    fresh_scores = (
        jnp.einsum("bsngd,btnd->bsngt", qb, knew, preferred_element_type=jnp.float32)
        * adapter_factor
    )
    cache_mask = (jnp.arange(slots)[None, :] < lengths[:, None])[:, None, None, None, :]
    fresh_mask = (jnp.arange(steps)[None, :] <= jnp.arange(steps)[:, None])[None, :, None, None, :]
    cache_scores = jnp.where(cache_mask, cache_scores, -1e30)
    fresh_scores = jnp.where(fresh_mask, fresh_scores, -1e30)
    top = jnp.maximum(jnp.max(cache_scores, axis=-1), jnp.max(fresh_scores, axis=-1))
    cache_exp = jnp.exp(cache_scores - top[..., None])
    fresh_exp = jnp.exp(fresh_scores - top[..., None])
    total = jnp.sum(cache_exp, axis=-1) + jnp.sum(fresh_exp, axis=-1)
    cache_prob = (cache_exp / total[..., None]).astype(jnp.bfloat16)
    fresh_prob = (fresh_exp / total[..., None]).astype(jnp.bfloat16)
    combined_output = jnp.einsum(
        "bsngc,bncd->bsngd", cache_prob, values, preferred_element_type=jnp.float32
    )
    combined_output = combined_output + jnp.einsum(
        "bsngt,btnd->bsngd", fresh_prob, vnew, preferred_element_type=jnp.float32
    )
    return combined_output.astype(jnp.bfloat16).reshape(rows * steps, kv_heads * group * head_size)


def per_device(
    acts,
    cotangent,
    out_weight,
    old_a,
    old_b,
    master_a,
    master_b,
    moment_a,
    moment_b,
    second_a,
    second_b,
    key_cache,
    value_cache,
    lengths,
    new_query,
    new_key,
    new_value,
):
    rank = old_a.shape[2]
    token_rows = acts.shape[0]
    local_down_factor = old_a.reshape(-1, rank)
    acts_low = lax.psum(
        jnp.dot(acts, local_down_factor, preferred_element_type=jnp.float32), "tensor"
    ).astype(jnp.bfloat16)
    piece = lax.all_gather(cotangent, "tensor", axis=1, tiled=True)
    w_cols = out_weight
    dims = (((1,), (1,)), ((), ()))
    backward_product = lax.dot_general(piece, w_cols, dims, preferred_element_type=jnp.float32)
    passed_down = lax.dot_general(piece, old_b, dims, preferred_element_type=jnp.float32)
    backward_product, passed_down = (backward_product, passed_down)
    passed_up_factor = passed_down.astype(jnp.bfloat16)
    attention_output_gradient = (
        backward_product
        + adapter_scale
        * jnp.dot(passed_up_factor, local_down_factor.T, preferred_element_type=jnp.float32)
    ).astype(jnp.bfloat16)
    adapter_factor = adapter_scale / (token_rows * lax.axis_size("dp"))
    rows_dims = (((0,), (0,)), ((), ()))
    grad_a = (
        adapter_factor
        * lax.dot_general(acts, passed_up_factor, rows_dims, preferred_element_type=jnp.float32)
    ).reshape(old_a.shape)
    grad_b = adapter_factor * lax.dot_general(
        acts_low, cotangent, rows_dims, preferred_element_type=jnp.float32
    )
    share_a, share_b = (
        lax.psum_scatter(grad_a, "dp", scatter_dimension=1, tiled=True),
        lax.psum_scatter(grad_b, "dp", scatter_dimension=0, tiled=True),
    )
    new_a, mom_a, sec_a = adam_step(master_a, moment_a, second_a, share_a)
    new_b, mom_b, sec_b = adam_step(master_b, moment_b, second_b, share_b)
    factor_a, factor_b = (
        lax.all_gather(new_a.astype(jnp.bfloat16), "dp", axis=1, tiled=True),
        lax.all_gather(new_b.astype(jnp.bfloat16), "dp", axis=0, tiled=True),
    )
    attended = attend_block(new_query, key_cache, value_cache, lengths, new_key, new_value)
    partial_low = jnp.dot(attended, factor_a.reshape(-1, rank), preferred_element_type=jnp.float32)
    col_dims = (((0,), (1,)), ((), ()))
    w_cols = out_weight
    combined_output = lax.psum_scatter(
        lax.dot_general(w_cols, attended, col_dims, preferred_element_type=jnp.float32),
        "tensor",
        scatter_dimension=0,
        tiled=True,
    )
    reduced_rank_input = lax.psum(partial_low, "tensor")
    combined_output = combined_output + adapter_scale * lax.dot_general(
        factor_b.astype(jnp.float32), reduced_rank_input, col_dims, precision=lax.Precision.HIGHEST
    )
    return (
        attention_output_gradient,
        new_a,
        new_b,
        mom_a,
        mom_b,
        sec_a,
        sec_b,
        combined_output.astype(jnp.bfloat16),
    )


def solution(mesh):
    return jax.shard_map(
        per_device,
        mesh=mesh,
        in_specs=(
            P("dp", "tensor"),
            P("dp", "tensor"),
            P("tensor", None),
            P("tensor", None, None),
            P(),
            P("tensor", "dp", None),
            P("dp", "tensor"),
            P("tensor", "dp", None),
            P("dp", "tensor"),
            P("tensor", "dp", None),
            P("dp", "tensor"),
            P("dp", "tensor", None, None),
            P("dp", "tensor", None, None),
            P("dp"),
            P("dp", None, "tensor"),
            P("dp", None, "tensor"),
            P("dp", None, "tensor"),
        ),
        out_specs=(
            P("dp", "tensor"),
            P("tensor", "dp", None),
            P("dp", "tensor"),
            P("tensor", "dp", None),
            P("dp", "tensor"),
            P("tensor", "dp", None),
            P("dp", "tensor"),
            P("tensor", "dp"),
        ),
        check_vma=False,
    )
```

profile of v0, /device:TPU:1, one launch (start us, length us, event | category | flops | bytes accessed | tf_op | source)
XLA Modules:
  0.0 557.0 jit_solution(3785150569864919158)
XLA Ops:
  7.2 0.7 all-gather.3.cloned.1.call-update
  8.0 1.1 reshape.131
  9.1 0.9 iota_compare_fusion
  9.9 3.5 fusion.58
  13.5 1.1 fusion.57
  14.7 0.7 fusion.30
  15.5 1.1 fusion.29
  16.6 0.8 add.72
  17.3 0.2 fusion.46
  17.5 31.2 %psum.14 = bf16[256,64]{0,1:T(8,128)(2,1)S(1)} all-reduce(f32[256,64]{0,1:T(8,128)S(1)} %fusion.46), channel_id=1, replica_groups=mesh['dp'=32,'tensor'=8] {'tensor'}, use_global_device_ids=true, to_apply=%region_1.0 | all-reduce | flops 16384 | bytes 98304 | tf_op jit(solution)/shard_map/psum | solution.py:82
  48.8 0.8 convolution_multiply_fusion.3
  49.6 2.9 fusion.34
  52.5 3.6 all-gather.3.cloned.1.call-done
  56.1 2.7 convolution_convert_fusion
  58.7 0.6 copy-done.5
  59.3 0.2 fusion.21
  59.5 0.8 copy.69
  60.5 2.5 fusion.16
  63.0 0.6 dynamic-slice
  64.2 273.5 %all-reduce.8.cloned.1.call-done = (f32[4,128,64]{2,1,0:T(8,128)}, f32[64,640]{1,0:T(8,128)}) async-done(((f32[4,128,64]{2,1,0:T(8,128)}, f32[64,640]{1,0:T(8,128)}), (f32[4,128,64]{2,1,0:T(8,128)}, f32[64,640]{1,0:T(8,128)})) %all-reduce.8.cloned.1.call-update) | async-done | bytes 294928
  337.7 1.3 fusion.54
  339.1 41.6 %all_gather.11 = bf16[4,128,64]{2,0,1:T(4,128)(2,1)S(1)} all-gather(bf16[4,4,64]{2,0,1:T(4,128)(2,1)S(1)} %copy.59), channel_id=1, replica_groups=mesh['dp'=32,'tensor'=8] {'dp'}, dimensions={1}, use_global_device_ids=true | all-gather | bytes 67584 | tf_op jit(solution)/shard_map/all_gather | solution.py:113
  380.8 0.9 fusion.31
  381.8 7.8 %convolution_bitcast_fusion = f32[5120,384]{0,1:T(8,128)} fusion(bf16[512,5120]{1,0:T(8,128)(2,1)} %param.19, bf16[48,8,4,128]{3,2,1,0:T(4,128)(2,1)S(1)} %bitcast.106), kind=kOutput, calls=%fused_computation | convolution fusion | flops 2013265920 | bytes 13500416 | tf_op jit(solution)/shard_map/dot_general | solution.py:121
  390.3 4.9 fusion.59
  395.2 1.0 fusion.20
  396.2 1.4 convert_bitcast_fusion
  397.5 41.8 %all-gather = bf16[32,2,640]{2,1,0:T(2,128)(2,1)S(1)} all-gather(bf16[1,2,640]{2,1,0:T(2,128)(2,1)S(1)} %get-tuple-element.46), channel_id=1, replica_groups=mesh['dp'=32,'tensor'=8] {'dp'}, dimensions={0}, use_global_device_ids=true | all-gather | bytes 84480 | tf_op jit(solution)/shard_map/all_gather | solution.py:114
  439.4 10.9 %all-reduce.6.cloned.1.call-done = f32[384,64]{0,1:T(8,128)} async-done(((f32[384,64]{0,1:T(8,128)}), f32[384,64]{0,1:T(8,128)}) %all-reduce.6.cloned.1.call-update) | async-done | bytes 98320 | tf_op jit(solution)/shard_map/psum | solution.py:126
  450.3 97.3 %reduce-scatter.3.cloned.1.call-done = f32[640,384]{0,1:T(8,128)} async-done(((f32[5120,384]{0,1:T(8,128)}), f32[640,384]{0,1:T(8,128)}) %reduce-scatter.3.cloned.1.call-update) | async-done | bytes 983056 | tf_op jit(solution)/shard_map/reduce_scatter | solution.py:120
  547.6 1.9 fusion.15
  549.5 1.0 copy.62
  (45 shorter events, 0.5 us)
Async XLA Ops:
  7.2 53.3 %copy-start = (bf16[128,1,48,128]{3,2,1,0:T(8,128)(2,1)S(1)}, bf16[128,1,48,128]{3,2,1,0:T(8,128)(2,1)}, u32[]{:S(2)}) copy-start(bf16[128,1,48,128]{3,2,1,0:T(8,128)(2,1)} %param.29) | copy-start | bytes 4718596
  7.2 48.9 %all-gather.3.cloned.1.call-start = ((), (), s32[]{:S(2)}) async-start(), calls=%async_computation.1 | async-start | bytes 2949120 | tf_op jit(solution)/shard_map/all_gather | solution.py:85
  7.9 329.8 %all-reduce.8.cloned.1.call-start = ((), (), s32[]{:S(2)}) async-start(), calls=%async_computation.4 | async-start | bytes 851968
  9.1 4.4 copy-start.15
  13.5 2.0 copy-start.3
  14.6 2.7 copy-start.2
  14.6 2.7 copy-start.7
  14.7 34.1 %copy-start.1 = (bf16[256,640]{1,0:T(8,128)(2,1)S(1)}, bf16[256,640]{1,0:T(8,128)(2,1)}, u32[]{:S(2)}) copy-start(bf16[256,640]{1,0:T(8,128)(2,1)} %param.18) | copy-start | bytes 983044
  49.6 6.5 %copy-start.4 = (bf16[64,5120]{1,0:T(8,128)(2,1)S(1)}, bf16[64,5120]{1,0:T(8,128)(2,1)}, u32[]{:S(2)}) copy-start(bf16[64,5120]{1,0:T(8,128)(2,1)} %param.21) | copy-start | bytes 1966084
  58.7 0.6 copy-start.5
  60.4 2.6 copy-start.16
  60.4 277.3 %copy-start.9 = (f32[4,4,64]{2,1,0:T(4,128)S(1)}, f32[4,4,64]{2,1,0:T(4,128)}, u32[]{:S(2)}) copy-start(f32[4,4,64]{2,1,0:T(4,128)} %param.22) | copy-start | bytes 12292
  60.4 277.3 %copy-start.10 = (f32[4,4,64]{2,1,0:T(4,128)S(1)}, f32[4,4,64]{2,1,0:T(4,128)}, u32[]{:S(2)}) copy-start(f32[4,4,64]{2,1,0:T(4,128)} %param.24) | copy-start | bytes 12292
  60.4 277.3 %copy-start.11 = (f32[4,4,64]{2,1,0:T(4,128)S(1)}, f32[4,4,64]{2,1,0:T(4,128)}, u32[]{:S(2)}) copy-start(f32[4,4,64]{2,1,0:T(4,128)} %param.26) | copy-start | bytes 12292
  60.4 389.9 %all-reduce.6.cloned.1.call-start = ((), (), s32[]{:S(2)}) async-start(), calls=%async_computation.3 | async-start | bytes 196608 | tf_op jit(solution)/shard_map/psum | solution.py:126
  381.8 165.8 %reduce-scatter.3.cloned.1.call-start = ((), (), s32[]{:S(2)}) async-start(), calls=%async_computation.2 | async-start | bytes 8847360 | tf_op jit(solution)/shard_map/reduce_scatter | solution.py:120
  390.3 4.9 copy-start.6
  390.3 4.9 copy-start.8
  390.3 5.9 %copy-start.12 = (f32[2,640]{1,0:T(2,128)S(1)}, f32[2,640]{1,0:T(2,128)}, u32[]{:S(2)}) copy-start(f32[2,640]{1,0:T(2,128)} %param.23) | copy-start | bytes 15364
  390.3 5.9 %copy-start.13 = (f32[2,640]{1,0:T(2,128)S(1)}, f32[2,640]{1,0:T(2,128)}, u32[]{:S(2)}) copy-start(f32[2,640]{1,0:T(2,128)} %param.25) | copy-start | bytes 15364
  390.3 5.9 %copy-start.14 = (f32[2,640]{1,0:T(2,128)S(1)}, f32[2,640]{1,0:T(2,128)}, u32[]{:S(2)}) copy-start(f32[2,640]{1,0:T(2,128)} %param.27) | copy-start | bytes 15364
Sparse Core Ops, SparseCore 0:
  9.8 46.2 all-gather.2
  60.5 277.1 all-reduce.7
  381.9 68.3 all-reduce.5
  452.7 94.8 reduce-scatter.2
where the time goes:
time: 557 us
  waiting for transfers between devices  386 us (69%)
  blocking collectives  115 us (21%)
  matrix products  30.2 us (5%)
  between operations  15.3 us (3%)
  other arithmetic  6.21 us (1%)
    unnamed x5, waiting for transfers between devices  274 us
    reduce_scatter x1, waiting for transfers between devices, per_device(): lax.psum_scatter(lax.dot_general(w_cols, attended, col_dims, preferred_el...  97.3 us
    all_gather x1, blocking collectives, per_device(): lax.all_gather(new_b.astype(jnp.bfloat16), 'dp', axis=0, tiled=True)  41.8 us
    all_gather x1, blocking collectives, per_device(): lax.all_gather(new_a.astype(jnp.bfloat16), 'dp', axis=1, tiled=True)  41.6 us
    psum x1, blocking collectives, per_device(): lax.psum(jnp.dot(acts, local_down_factor, preferred_element_type=jnp.floa...  31.2 us
  transfers between devices with their start and end apart: 4, of which 4 were waited for; matrix products, arithmetic and copies ran while one was open for 6% of the time, Pallas kernels for 0%

commit v1 on v0

v1 whole, which is shorter than its diff:
```python
import functools

import jax
import jax.numpy as jnp
from jax import lax
from jax.experimental import pallas as pl
from jax.experimental.pallas import tpu as pltpu
from jax.sharding import PartitionSpec as P

adapter_scale = 2.0
beta_one = 0.9
beta_two = 0.999
learn_rate = 0.01
decay_rate = 0.01
corr_one = 1.0 - 0.9**10
corr_two = 1.0 - 0.999**10
MESH = pl.DeviceIdType.MESH
f32 = jnp.float32
bf16 = jnp.bfloat16
NT = (((1,), (1,)), ((), ()))
NN = (((1,), (0,)), ((), ()))


def mm(a, b, dims=NN):
    return lax.dot_general(a, b, dims, preferred_element_type=f32)


def iota(shape, dim):
    return lax.broadcasted_iota(jnp.int32, shape, dim)


def onehot(hit):
    return jnp.where(hit, 1.0, 0.0).astype(f32).astype(bf16)


def adam_step(master, moment, second, grad):
    moment_new = beta_one * moment + (1.0 - beta_one) * grad
    second_new = beta_two * second + (1.0 - beta_two) * grad * grad
    update = moment_new / corr_one / (jnp.sqrt(second_new / corr_two) + 1e-08)
    return (master - learn_rate * (update + decay_rate * master), moment_new, second_new)


def kernel(
    acts_h, cot_h, w_h, olda_h, oldb_h,
    ma, mb, oa, ob, va, vb,
    key_h, val_h, len_ref, q_h, nk_h, nv_h,
    grad_o, nma_o, nmb_o, noa_o, nob_o, nva_o, nvb_o, out_o,
    acts, cot, w, olda, oldb, keys, vals, q, nk, nv,
    perma, spread, gather, permr, slotm, freshb, lencol,
    part, prs, lows, lowf, cgat, gacc,
    gst, gpeer, hsum, hrecv, ga_s, gb_s, fac,
    att, attp, att2, ysend, yown, yrecv, lsend, lrecv,
    lsem, s_prs, r_prs, s_pag, r_pag, s_cot, r_cot, s_core, r_core, s_dp, r_dp,
    s_fac, r_fac, s_fcore, r_fcore, s_y, r_y, s_low, r_low,
):
    dp = lax.axis_index("dp")
    t = lax.axis_index("tensor")
    chip = dp // 2
    core = dp % 2

    def tpeer(k):
        return (dp, (t + k) % 8)

    def cpeer(k):
        return (((chip + k) % 16) * 2 + core, t)

    corepeer = (chip * 2 + 1 - core, t)

    def remote(src, dst, ssem, rsem, dev):
        return pltpu.make_async_remote_copy(
            src_ref=src, dst_ref=dst, send_sem=ssem, recv_sem=rsem, device_id=dev, device_id_type=MESH
        )

    def drain(ref, sem):
        pltpu.make_async_copy(ref, ref, sem).wait()

    loads = [
        pltpu.make_async_copy(acts_h, acts, lsem.at[0]),
        pltpu.make_async_copy(cot_h, cot, lsem.at[1]),
        pltpu.make_async_copy(olda_h, olda, lsem.at[2]),
        pltpu.make_async_copy(oldb_h.at[:, pl.ds(pl.multiple_of(t * 640, 128), 640)], oldb, lsem.at[3]),
        pltpu.make_async_copy(q_h, q, lsem.at[4]),
        pltpu.make_async_copy(key_h, keys, lsem.at[5]),
        pltpu.make_async_copy(nk_h, nk, lsem.at[6]),
        pltpu.make_async_copy(val_h, vals, lsem.at[7]),
        pltpu.make_async_copy(nv_h, nv, lsem.at[8]),
    ]
    for j in range(8):
        loads.append(pltpu.make_async_copy(w_h.at[:, pl.ds(j * 640, 640)], w.at[j], lsem.at[9 + j]))
    for c in loads:
        c.start()

    bar = pltpu.get_barrier_semaphore()

    def sig_t(k, _):
        pl.semaphore_signal(bar, inc=1, device_id=tpeer(k), device_id_type=MESH)
        return 0

    def sig_c(k, _):
        pl.semaphore_signal(bar, inc=1, device_id=cpeer(k), device_id_type=MESH)
        return 0

    lax.fori_loop(1, 8, sig_t, 0)
    lax.fori_loop(1, 16, sig_c, 0)
    pl.semaphore_signal(bar, inc=1, device_id=corepeer, device_id_type=MESH)

    for c in loads[:4]:
        c.wait()
    low_p = mm(acts[:, 0:128], olda[0], NT)
    for h in range(1, 4):
        low_p += mm(acts[:, h * 128 : (h + 1) * 128], olda[h], NT)
    thr_p = mm(cot[...], oldb[...], NT)
    part[...] = jnp.concatenate([low_p, thr_p], axis=1).reshape(8, 32, 128)
    pl.semaphore_wait(bar, 23)

    def send_part(k, _):
        remote(part.at[(t + k) % 8], prs.at[7 - k], s_prs, r_prs, tpeer(k)).start()
        return 0

    lax.fori_loop(1, 8, send_part, 0)

    def send_cot(k, _):
        remote(cot, cgat.at[7 - k], s_cot, r_cot.at[7 - k], tpeer(k)).start()
        return 0

    lax.fori_loop(1, 8, send_cot, 0)

    prow, pcol = iota((512, 512), 0), iota((512, 512), 1)
    blk = prow >> 4
    perma[...] = onehot(
        pcol == (((prow >> 2) & 3) << 7) + (((blk & 15) * 2 + (blk >> 4)) << 2) + (prow & 3)
    )
    erow, ecol = iota((512, 320), 0), iota((512, 320), 1)
    blk = erow >> 4
    idx = erow & 15
    spread[...] = onehot(
        (idx < 10) & (ecol == ((idx >> 1) << 6) + ((blk & 15) * 2 + (blk >> 4)) * 2 + (idx & 1))
    )
    erow, ecol = iota((320, 512), 1), iota((320, 512), 0)
    blk = erow >> 4
    idx = erow & 15
    gather[...] = onehot(
        (idx < 10) & (ecol == ((idx >> 1) << 6) + ((blk & 15) * 2 + (blk >> 4)) * 2 + (idx & 1))
    )
    rj, rk = iota((384, 384), 0), iota((384, 384), 1)
    permr[...] = onehot((rj - 3 * (rk & 127)) == (rk >> 7))
    slot = iota((16, 768), 1) - 48 * iota((16, 768), 0)
    slotm[...] = jnp.where((slot >= 0) & (slot < 48), slot, 1000)
    fr, fc = iota((192, 48), 0), iota((192, 48), 1)
    freshb[...] = jnp.where(((fr & 15) == (fc & 15)) & ((fc >> 4) <= (fr >> 6)), 0.0, -1e30).astype(f32)
    diag = iota((128, 128), 0) == iota((128, 128), 1)
    lencol[...] = jnp.broadcast_to(
        jnp.sum(jnp.where(diag, len_ref[...].astype(f32), 0.0), axis=1, keepdims=True), (128, 128)
    )

    scale = f32(1.0) / jnp.sqrt(f32(128.0))

    def attend(g, _):
        rows = pl.ds(pl.multiple_of(g * 16, 16), 16)
        qg = jnp.concatenate(
            [q[s, rows, h * 128 : (h + 1) * 128] for s in range(3) for h in range(4)], axis=0
        )
        kg = keys[rows].reshape(768, 128)
        vg = vals[rows].reshape(768, 128)
        nkg = jnp.concatenate([nk[s, rows, :] for s in range(3)], axis=0)
        nvg = jnp.concatenate([nv[s, rows, :] for s in range(3)], axis=0)
        bias = jnp.where(slotm[...].astype(f32) < lencol[rows, 0:1], 0.0, -1e30).astype(f32)
        s1 = (mm(qg, kg, NT) * scale).reshape(12, 16, 768) + bias[None]
        s1 = s1.reshape(192, 768)
        s2 = mm(qg, nkg, NT) * scale + freshb[...]
        top = jnp.maximum(jnp.max(s1, axis=1, keepdims=True), jnp.max(s2, axis=1, keepdims=True))
        e1 = jnp.exp(s1 - top)
        e2 = jnp.exp(s2 - top)
        inv = 1.0 / (jnp.sum(e1, axis=1, keepdims=True) + jnp.sum(e2, axis=1, keepdims=True))
        o = mm((e1 * inv).astype(bf16), vg) + mm((e2 * inv).astype(bf16), nvg)
        o = o.astype(bf16)
        for s in range(3):
            for h in range(4):
                i = (s * 4 + h) * 16
                att[s, rows, h * 128 : (h + 1) * 128] = o[i : i + 16]
        return 0

    for c in loads[4:9]:
        c.wait()
    lax.fori_loop(0, 2, attend, 0)

    drain(prs, r_prs)
    tot = part[t]
    for k in range(7):
        tot += prs[k]
    lows[...] = tot.astype(bf16)
    lowf[t] = tot.astype(bf16)

    def send_low(k, _):
        remote(lows, lowf.at[t], s_pag, r_pag, tpeer(k)).start()
        return 0

    lax.fori_loop(1, 8, send_low, 0)
    lax.fori_loop(2, 4, attend, 0)
    drain(lowf.at[pl.ds(0, 7)], r_pag)

    both = lowf[...].reshape(256, 128)
    both_t = both.astype(f32).T.astype(bf16)
    ga_t = mm(both_t[64:128], acts[...]).astype(bf16)
    gb = mm(both_t[0:64], cot[...]).astype(bf16)
    ga = mm(perma[...], ga_t, NT)
    gb = jnp.concatenate([gb[:, c * 128 : (c + 1) * 128] for c in range(5)], axis=0)
    gb = mm(spread[...], gb)
    gst[:, 0:16, :] = gb.astype(bf16).reshape(32, 16, 128)
    gst[:, 16:32, :] = jnp.concatenate([ga, jnp.zeros_like(ga)], axis=1).astype(bf16).reshape(32, 16, 128)
    cc = remote(gst.at[pl.ds((1 - core) * 16, 16)], gpeer, s_core, r_core, corepeer)
    cc.start()
    cc.wait_recv()
    hsum[...] = (gst[pl.ds(core * 16, 16)].astype(f32) + gpeer[...].astype(f32)).astype(bf16)

    def send_share(k, _):
        remote(hsum.at[(chip + k) % 16], hrecv.at[15 - k], s_dp, r_dp, cpeer(k)).start()
        return 0

    lax.fori_loop(1, 16, send_share, 0)
    lax.fori_loop(4, 8, attend, 0)
    attp[...] = mm(permr[...], att[...].reshape(384, 512)).astype(bf16)
    att2[...] = mm(attp[...], perma[...], NT).astype(bf16)
    drain(hrecv, r_dp)

    share = hsum[chip].astype(f32)
    for k in range(15):
        share += hrecv[k].astype(f32)
    share = share * (adapter_scale / 8192.0)
    gb_s[...] = share[0:16]
    ga_s[...] = share[16:32]
    for h in range(4):
        r = slice(h * 4, h * 4 + 4)
        new_p, new_m, new_v = adam_step(ma[h], oa[h], va[h], ga_s[r, 0:64])
        nma_o[h], noa_o[h], nva_o[h] = new_p, new_m, new_v
        ga_s[r, 0:64] = new_p
    for c in range(5):
        r = slice(c * 2, c * 2 + 2)
        l = slice(c * 128, (c + 1) * 128)
        new_p, new_m, new_v = adam_step(mb[:, l], ob[:, l], vb[:, l], gb_s[r, :])
        nmb_o[:, l], nob_o[:, l], nvb_o[:, l] = new_p, new_m, new_v
        gb_s[r, :] = new_p
    mine = core * 16 + chip
    fac[mine] = jnp.concatenate([gb_s[...], ga_s[...]], axis=0).astype(bf16)

    def send_fac(k, _):
        remote(fac.at[mine], fac.at[mine], s_fac, r_fac, cpeer(k)).start()
        return 0

    lax.fori_loop(1, 16, send_fac, 0)

    for c in loads[9:]:
        c.wait()

    def project(k, _):
        ysend[k - 1] = mm(attp[...], w[(t + k) % 8]).astype(bf16)
        remote(ysend.at[k - 1], yrecv.at[7 - k], s_y, r_y.at[7 - k], tpeer(k)).start()
        return 0

    lax.fori_loop(1, 8, project, 0)
    yown[...] = mm(attp[...], w[t])

    half = pl.ds(core * 16, 16)
    drain(fac.at[pl.ds(0, 15)], r_fac)
    fc = remote(fac.at[half], fac.at[half], s_fcore, r_fcore, corepeer)
    fc.start()
    thr = both[:, 64:128]
    add = [mm(thr, olda[h]) for h in range(4)]
    gacc[...] = adapter_scale * jnp.concatenate(add, axis=1) + mm(cot[...], w[t], NT)
    fc.wait_recv()

    a_new = fac[:, 16:32, :].reshape(512, 128)
    low = mm(att2[...], a_new)[:, 0:64]
    low = jnp.concatenate([low[0:192], low[192:384]], axis=1)
    lsend[...] = low.astype(bf16)

    def send_l(k, _):
        remote(lsend, lrecv.at[7 - k], s_low, r_low, tpeer(k)).start()
        return 0

    lax.fori_loop(1, 8, send_l, 0)
    b_new = mm(gather[...], fac[:, 0:16, :].reshape(512, 128)).astype(bf16)
    b_new = jnp.concatenate([b_new[c * 64 : (c + 1) * 64] for c in range(5)], axis=1)

    def accumulate(k, _):
        drain(cgat.at[7 - k], r_cot.at[7 - k])
        gacc[...] += mm(cgat[7 - k], w[(t + 8 - k) % 8], NT)
        return 0

    lax.fori_loop(1, 8, accumulate, 0)
    grad_o[...] = gacc[...].astype(bf16)

    drain(lrecv, r_low)
    for k in range(7):
        low += lrecv[k].astype(f32)
    low = jnp.concatenate([low[:, 0:64], low[:, 64:128]], axis=0)
    hi = low.astype(bf16)
    lo = (low - hi.astype(f32)).astype(bf16)
    yown[...] += adapter_scale * (mm(hi, b_new) + mm(lo, b_new))

    def collect(k, _):
        drain(yrecv.at[7 - k], r_y.at[7 - k])
        yown[...] += yrecv[7 - k].astype(f32)
        return 0

    lax.fori_loop(1, 8, collect, 0)
    out_o[...] = yown[...].T.astype(bf16)

    cc.wait_send()
    fc.wait_send()
    drain(prs, s_prs)
    drain(lowf.at[pl.ds(0, 7)], s_pag)
    drain(cgat, s_cot)
    drain(hrecv, s_dp)
    drain(fac.at[pl.ds(0, 15)], s_fac)
    drain(yrecv, s_y)
    drain(lrecv, s_low)


def per_device(
    acts, cotangent, out_weight, old_a, old_b, master_a, master_b, moment_a, moment_b, second_a, second_b,
    key_cache, value_cache, lengths, new_query, new_key, new_value,
):
    hbm = pl.BlockSpec(memory_space=pl.ANY)
    vmem = pl.BlockSpec(memory_space=pltpu.VMEM)
    dma = pltpu.SemaphoreType.DMA
    V = pltpu.VMEM
    shp = jax.ShapeDtypeStruct
    return pl.pallas_call(
        kernel,
        out_shape=(
            shp((256, 512), bf16), shp((4, 4, 64), f32), shp((2, 640), f32), shp((4, 4, 64), f32),
            shp((2, 640), f32), shp((4, 4, 64), f32), shp((2, 640), f32), shp((640, 384), bf16),
        ),
        in_specs=[hbm] * 5 + [vmem] * 6 + [hbm] * 2 + [vmem] + [hbm] * 3,
        out_specs=(vmem,) * 8,
        scratch_shapes=[
            V((256, 512), bf16), V((256, 640), bf16), V((8, 512, 640), bf16), V((4, 64, 128), bf16),
            V((64, 640), bf16), V((128, 48, 128), bf16), V((128, 48, 128), bf16), V((3, 128, 512), bf16),
            V((3, 128, 128), bf16), V((3, 128, 128), bf16),
            V((512, 512), bf16), V((512, 320), bf16), V((320, 512), bf16), V((384, 384), bf16),
            V((16, 768), jnp.int32), V((192, 48), f32), V((128, 128), f32),
            V((8, 32, 128), f32), V((7, 32, 128), f32), V((32, 128), bf16), V((8, 32, 128), bf16),
            V((7, 256, 640), bf16), V((256, 512), f32),
            V((32, 32, 128), bf16), V((16, 32, 128), bf16), V((16, 32, 128), bf16), V((15, 32, 128), bf16),
            V((16, 128), f32), V((16, 128), f32), V((32, 32, 128), bf16),
            V((3, 128, 512), bf16), V((384, 512), bf16), V((384, 512), bf16),
            V((7, 384, 640), bf16), V((384, 640), f32), V((7, 384, 640), bf16),
            V((192, 128), bf16), V((7, 192, 128), bf16),
            dma((17,)), dma, dma, dma, dma, dma, dma((7,)), dma, dma, dma, dma,
            dma, dma, dma, dma, dma, dma((7,)), dma, dma,
        ],
        compiler_params=pltpu.CompilerParams(
            collective_id=0, has_side_effects=True, vmem_limit_bytes=56 << 20
        ),
        cost_estimate=pl.CostEstimate(flops=4 << 30, bytes_accessed=12 << 20, transcendentals=1 << 20),
        name="update_and_decode",
    )(
        acts, cotangent, out_weight, old_a.swapaxes(1, 2), old_b,
        master_a, master_b, moment_a, moment_b, second_a, second_b,
        key_cache.reshape(128, 48, 128), value_cache.reshape(128, 48, 128), lengths.reshape(1, 128),
        new_query.swapaxes(0, 1), new_key.swapaxes(0, 1), new_value.swapaxes(0, 1),
    )


def solution(mesh):
    return jax.shard_map(
        per_device,
        mesh=mesh,
        in_specs=(
            P("dp", "tensor"),
            P("dp", "tensor"),
            P("tensor", None),
            P("tensor", None, None),
            P(),
            P("tensor", "dp", None),
            P("dp", "tensor"),
            P("tensor", "dp", None),
            P("dp", "tensor"),
            P("tensor", "dp", None),
            P("dp", "tensor"),
            P("dp", "tensor", None, None),
            P("dp", "tensor", None, None),
            P("dp"),
            P("dp", None, "tensor"),
            P("dp", None, "tensor"),
            P("dp", None, "tensor"),
        ),
        out_specs=(
            P("dp", "tensor"),
            P("tensor", "dp", None),
            P("dp", "tensor"),
            P("tensor", "dp", None),
            P("dp", "tensor"),
            P("tensor", "dp", None),
            P("dp", "tensor"),
            P("tensor", "dp"),
        ),
        check_vma=False,
    )
```

time: 557 us -> 143 us (0.26)
  waiting for transfers between devices: 386 us -> 0 us
  Pallas kernels: 0 us -> 130 us
  blocking collectives: 115 us -> 0 us
  matrix products: 30.2 us -> 0 us
  between operations: 15.3 us -> 0.65 us
  local copies, waits for them, and re-layouts: 4.36 us -> 11.3 us
  other arithmetic: 6.21 us -> 0 us
    unnamed x5 -> x0, waiting for transfers between devices: 274 us -> none
    pallas_call x0 -> x1, Pallas kernels: none -> 130 us  [per_device(): pl.pallas_call(kernel, out_shape=(shp((256, 512), bf16), shp((4, 4, 64),...]
    reduce_scatter x1 -> x0, waiting for transfers between devices: 97.3 us -> none  [per_device(): lax.psum_scatter(lax.dot_general(w_cols, attended, col_dims, preferred_el...]
    all_gather x2 -> x0, blocking collectives: 83.5 us -> none  [the longest x1 41.8 us: per_device(): lax.all_gather(new_b.astype(jnp.bfloat16), 'dp', axis=0, tiled=True)]
    psum x1 -> x0, blocking collectives: 31.2 us -> none  [per_device(): lax.psum(jnp.dot(acts, local_down_factor, preferred_element_type=jnp.floa...]
    dot_general x13 -> x0, matrix products: 30.2 us -> none  [the longest x1 7.75 us: per_device(): lax.dot_general(w_cols, attended, col_dims, preferred_element_type=jnp.fl...]
    psum x1 -> x0, waiting for transfers between devices: 10.9 us -> none  [per_device(): reduced_rank_input = lax.psum(partial_low, 'tensor')]
    unnamed x37 -> x8, local copies, waits for them, and re-layouts: 2.31 us -> 11.3 us
  transfers between devices with their start and end apart: 4 -> 0, of which waited for: 4 -> 0; matrix products, arithmetic and copies ran while one was open for 6% -> 0% of each run, Pallas kernels for 0% -> 0%
where the time goes in v1:
time: 143 us; the launch traced here: 142 us
  Pallas kernels  130 us (91%)
  local copies, waits for them, and re-layouts  11.3 us (8%)
    pallas_call x1, Pallas kernels, per_device(): pl.pallas_call(kernel, out_shape=(shp((256, 512), bf16), shp((4, 4, 64),...  130 us
    unnamed x8, local copies, waits for them, and re-layouts  11.3 us

profile of v1, /device:TPU:1, one launch (start us, length us, event | category | flops | bytes accessed | tf_op | source)
XLA Modules:
  0.0 141.6 jit_solution(4286233718280057091)
XLA Ops:
  0.6 129.7 %update_and_decode.1 = (bf16[256,512]{1,0:T(8,128)(2,1)}, f32[4,4,64]{2,1,0:T(4,128)}, f32[2,640]{1,0:T(2,128)}, f32[4,4,64]{2,1,0:T(4,128)}, f32[2,640]{1,0:T(2...) custom-call(bf16[256,512]{1,0:T(8,128)(2,1)} %acts_h.1, bf16[256,640]{1,0:T(8,128)(2,1)} %cot_h.1, ...), custom_call_target="tpu_custom_call" | custom-call | flops 4294967296 | bytes 12582912 | tf_op jit(solution)/shard_map/update_and_decode/pallas_call | solution.py:329
  130.4 1.7 %copy.33 = bf16[256,512]{1,0:T(8,128)(2,1)} copy(bf16[256,512]{1,0:T(8,128)(2,1)} %get-tuple-element.16) | data formatting | bytes 524288
  132.0 1.3 copy.34
  133.3 1.3 copy.35
  134.6 1.3 copy.36
  135.9 1.3 copy.37
  137.2 1.3 copy.38
  138.5 1.3 copy.39
  139.8 1.9 %copy.40 = bf16[640,384]{1,0:T(8,128)(2,1)} copy(bf16[640,384]{1,0:T(8,128)(2,1)} %get-tuple-element.23) | data formatting | bytes 983040

commit v2 on v1

--- a/solution.py
+++ b/solution.py
@@ -49,14 +49,16 @@
     perma, spread, gather, permr, slotm, freshb, lencol,
     part, prs, lows, lowf, cgat, gacc,
     gst, gpeer, hsum, hrecv, ga_s, gb_s, fac,
-    att, attp, att2, ysend, yown, yrecv, lsend, lrecv,
-    lsem, s_prs, r_prs, s_pag, r_pag, s_cot, r_cot, s_core, r_core, s_dp, r_dp,
-    s_fac, r_fac, s_fcore, r_fcore, s_y, r_y, s_low, r_low,
+    att, attp, att2, yb, yown, za, far, fin, zbr, lsend, lrecv,
+    lsem, s_prs, r_prs, s_pag, r_pag, s_ag, r_ag, s_gz, r_gz, s_core, r_core, s_dp, r_dp,
+    s_fac, r_fac, s_fcore, r_fcore, s_za, r_za, s_p1, r_p1, s_raw, r_raw, s_p2, r_p2, s_zb, r_zb, s_low, r_low,
 ):
     dp = lax.axis_index("dp")
     t = lax.axis_index("tensor")
     chip = dp // 2
     core = dp % 2
+    z = t // 4
+    y = t % 4
 
     def tpeer(k):
         return (dp, (t + k) % 8)
@@ -65,6 +67,12 @@
         return (((chip + k) % 16) * 2 + core, t)
 
     corepeer = (chip * 2 + 1 - core, t)
+    twin = (1 - z) * 4 + y
+    zdev = (dp, twin)
+    ynext = ((y + 1) % 4, (y + 3) % 4)
+    yfar = (y + 2) % 4
+    ydev = tuple((dp, z * 4 + n) for n in ynext)
+    yprev = (ynext[1], ynext[0])
 
     def remote(src, dst, ssem, rsem, dev):
         return pltpu.make_async_remote_copy(
@@ -119,11 +127,27 @@
 
     lax.fori_loop(1, 8, send_part, 0)
 
-    def send_cot(k, _):
-        remote(cot, cgat.at[7 - k], s_cot, r_cot.at[7 - k], tpeer(k)).start()
-        return 0
-
-    lax.fori_loop(1, 8, send_cot, 0)
+    def half(h):
+        return pl.ds(h * 128, 128)
+
+    def gather_own(h):
+        remote(cot.at[half(h)], cgat.at[t, half(h)], s_gz, r_gz.at[h], zdev).start()
+        for d in range(2):
+            remote(cot.at[half(h)], cgat.at[t, half(h)], s_ag, r_ag.at[d, h], ydev[d]).start()
+
+    def gather_twin(h):
+        drain(cgat.at[twin, half(h)], r_gz.at[h])
+        for d in range(2):
+            remote(cgat.at[twin, half(h)], cgat.at[twin, half(h)], s_ag, r_ag.at[d, 2 + h], ydev[d]).start()
+
+    def gather_relay(which):
+        for d in range(2):
+            src = (z if which == 0 else 1 - z) * 4 + yprev[d]
+            blk = cgat.at[src, half(d)]
+            drain(blk, r_ag.at[d, which * 2 + d])
+            remote(blk, blk, s_ag, r_ag.at[d, 4 + which], ydev[d]).start()
+
+    gather_own(0)
 
     prow, pcol = iota((512, 512), 0), iota((512, 512), 1)
     blk = prow >> 4
@@ -142,8 +166,8 @@
     gather[...] = onehot(
         (idx < 10) & (ecol == ((idx >> 1) << 6) + ((blk & 15) * 2 + (blk >> 4)) * 2 + (idx & 1))
     )
-    rj, rk = iota((384, 384), 0), iota((384, 384), 1)
-    permr[...] = onehot((rj - 3 * (rk & 127)) == (rk >> 7))
+    rj, rk = iota((192, 192), 0), iota((192, 192), 1)
+    permr[...] = onehot((rj - 3 * (rk & 63)) == (rk >> 6))
     slot = iota((16, 768), 1) - 48 * iota((16, 768), 0)
     slotm[...] = jnp.where((slot >= 0) & (slot < 48), slot, 1000)
     fr, fc = iota((192, 48), 0), iota((192, 48), 1)
@@ -180,9 +204,61 @@
                 att[s, rows, h * 128 : (h + 1) * 128] = o[i : i + 16]
         return 0
 
+    rows_a = pl.ds(0, 192)
+    rows_b = pl.ds(192, 192)
+
+    def order_rows(i):
+        block = att[:, i * 64 : (i + 1) * 64, :].reshape(192, 512)
+        attp[pl.ds(i * 192, 192)] = mm(permr[...], block).astype(bf16)
+
+    def project(rows):
+        def one(j, _):
+            yb[j, rows] = mm(attp[rows], w[j]).astype(bf16)
+            return 0
+
+        return one
+
+    this, other = z * 4, (1 - z) * 4
+
+    def send_za(j):
+        remote(yb.at[other + j, rows_a], za.at[j], s_za, r_za.at[j], zdev).start()
+
+    half_rows = 96
+    classes = ((0, z), (192, z), (192, 1 - z))
+
+    def part_of(c, owner, h):
+        r0, plane = classes[c]
+        return yb.at[plane * 4 + owner, pl.ds(r0 + h * half_rows, half_rows)]
+
+    def y_far(c):
+        for d in range(2):
+            remote(part_of(c, yfar, d), far.at[c, d], s_p1.at[c], r_p1.at[c, d], ydev[d]).start()
+
+    def y_raw(c):
+        for d in range(2):
+            remote(
+                part_of(c, ynext[d], 1 - d), fin.at[c, d, 1 - d], s_raw.at[c], r_raw.at[c, d], ydev[d]
+            ).start()
+
+    def y_relay(c):
+        for d in range(2):
+            drain(far.at[c, d], r_p1.at[c, d])
+            blk = part_of(c, ynext[d], d)
+            blk[...] = (blk[...].astype(f32) + far[c, d].astype(f32)).astype(bf16)
+            remote(blk, fin.at[c, d, d], s_p2.at[c], r_p2.at[c, d], ydev[d]).start()
+
+    def y_total(c, h):
+        return fin[c, 0, h].astype(f32) + fin[c, 1, h].astype(f32)
+
+    def y_wait(c):
+        for d in range(2):
+            drain(fin.at[c, d, 1 - d], r_raw.at[c, d])
+            drain(fin.at[c, d, d], r_p2.at[c, d])
+
     for c in loads[4:9]:
         c.wait()
-    lax.fori_loop(0, 2, attend, 0)
+    lax.fori_loop(0, 4, attend, 0)
+    order_rows(0)
 
     drain(prs, r_prs)
     tot = part[t]
@@ -196,7 +272,14 @@
         return 0
 
     lax.fori_loop(1, 8, send_low, 0)
-    lax.fori_loop(2, 4, attend, 0)
+    gather_own(1)
+    for c in loads[9:]:
+        c.wait()
+    lax.fori_loop(other, other + 4, project(rows_a), 0)
+    send_za(0)
+    gather_twin(0)
+    lax.fori_loop(4, 6, attend, 0)
+
     drain(lowf.at[pl.ds(0, 7)], r_pag)
 
     both = lowf[...].reshape(256, 128)
@@ -210,6 +293,8 @@
     gst[:, 16:32, :] = jnp.concatenate([ga, jnp.zeros_like(ga)], axis=1).astype(bf16).reshape(32, 16, 128)
     cc = remote(gst.at[pl.ds((1 - core) * 16, 16)], gpeer, s_core, r_core, corepeer)
     cc.start()
+
+    lax.fori_loop(6, 8, attend, 0)
     cc.wait_recv()
     hsum[...] = (gst[pl.ds(core * 16, 16)].astype(f32) + gpeer[...].astype(f32)).astype(bf16)
 
@@ -218,9 +303,18 @@
         return 0
 
     lax.fori_loop(1, 16, send_share, 0)
-    lax.fori_loop(4, 8, attend, 0)
-    attp[...] = mm(permr[...], att[...].reshape(384, 512)).astype(bf16)
+    gather_twin(1)
+    send_za(1)
+    order_rows(1)
+    lax.fori_loop(other, other + 4, project(rows_b), 0)
+    lax.fori_loop(this, this + 4, project(rows_b), 0)
+    gather_relay(0)
+    y_far(2)
+    y_far(1)
+    lax.fori_loop(this, this + 4, project(rows_a), 0)
+    yown[...] = mm(attp[...], w[t])
     att2[...] = mm(attp[...], perma[...], NT).astype(bf16)
+
     drain(hrecv, r_dp)
 
     share = hsum[chip].astype(f32)
@@ -248,25 +342,23 @@
         return 0
 
     lax.fori_loop(1, 16, send_fac, 0)
-
-    for c in loads[9:]:
-        c.wait()
-
-    def project(k, _):
-        ysend[k - 1] = mm(attp[...], w[(t + k) % 8]).astype(bf16)
-        remote(ysend.at[k - 1], yrecv.at[7 - k], s_y, r_y.at[7 - k], tpeer(k)).start()
-        return 0
-
-    lax.fori_loop(1, 8, project, 0)
-    yown[...] = mm(attp[...], w[t])
-
-    half = pl.ds(core * 16, 16)
-    drain(fac.at[pl.ds(0, 15)], r_fac)
-    fc = remote(fac.at[half], fac.at[half], s_fcore, r_fcore, corepeer)
-    fc.start()
+    send_za(2)
+    send_za(3)
+    gather_relay(1)
+
     thr = both[:, 64:128]
     add = [mm(thr, olda[h]) for h in range(4)]
     gacc[...] = adapter_scale * jnp.concatenate(add, axis=1) + mm(cot[...], w[t], NT)
+    gacc[...] += mm(cgat[twin], w[twin], NT)
+
+    y_relay(2)
+    y_raw(2)
+    y_relay(1)
+
+    mycore = pl.ds(core * 16, 16)
+    drain(fac.at[pl.ds(0, 15)], r_fac)
+    fc = remote(fac.at[mycore], fac.at[mycore], s_fcore, r_fcore, corepeer)
+    fc.start()
     fc.wait_recv()
 
     a_new = fac[:, 16:32, :].reshape(512, 128)
@@ -282,13 +374,39 @@
     b_new = mm(gather[...], fac[:, 0:16, :].reshape(512, 128)).astype(bf16)
     b_new = jnp.concatenate([b_new[c * 64 : (c + 1) * 64] for c in range(5)], axis=1)
 
+    for j in range(4):
+        drain(za.at[j], r_za.at[j])
+        blk = yb.at[this + j, rows_a]
+        blk[...] = (blk[...].astype(f32) + za[j].astype(f32)).astype(bf16)
+    yown[rows_a] += za[y].astype(f32)
+    y_far(0)
+    y_raw(1)
+
+    for d in range(2):
+        for h in range(2):
+            if h != d:
+                drain(cgat.at[this + yprev[d], half(h)], r_ag.at[d, h])
+                drain(cgat.at[other + yprev[d], half(h)], r_ag.at[d, 2 + h])
+        drain(cgat.at[this + yfar, half(d)], r_ag.at[d, 4])
+        drain(cgat.at[other + yfar, half(d)], r_ag.at[d, 5])
+
     def accumulate(k, _):
-        drain(cgat.at[7 - k], r_cot.at[7 - k])
-        gacc[...] += mm(cgat[7 - k], w[(t + 8 - k) % 8], NT)
-        return 0
-
-    lax.fori_loop(1, 8, accumulate, 0)
+        src = jnp.where(k < 3, z, 1 - z) * 4 + (y + 1 + k % 3) % 4
+        gacc[...] += mm(cgat[src], w[src], NT)
+        return 0
+
+    lax.fori_loop(0, 6, accumulate, 0)
     grad_o[...] = gacc[...].astype(bf16)
+
+    y_wait(2)
+    for h in range(2):
+        blk = part_of(2, y, h)
+        blk[...] = (blk[...].astype(f32) + y_total(2, h)).astype(bf16)
+    zb = remote(yb.at[twin, rows_b], zbr, s_zb, r_zb, zdev)
+    zb.start()
+
+    y_relay(0)
+    y_raw(0)
 
     drain(lrecv, r_low)
     for k in range(7):
@@ -298,23 +416,36 @@
     lo = (low - hi.astype(f32)).astype(bf16)
     yown[...] += adapter_scale * (mm(hi, b_new) + mm(lo, b_new))
 
-    def collect(k, _):
-        drain(yrecv.at[7 - k], r_y.at[7 - k])
-        yown[...] += yrecv[7 - k].astype(f32)
-        return 0
-
-    lax.fori_loop(1, 8, collect, 0)
+    y_wait(1)
+    for h in range(2):
+        yown[pl.ds(192 + h * half_rows, half_rows)] += y_total(1, h)
+    zb.wait_recv()
+    yown[rows_b] += zbr[...].astype(f32)
+    y_wait(0)
+    for h in range(2):
+        yown[pl.ds(h * half_rows, half_rows)] += y_total(0, h)
     out_o[...] = yown[...].T.astype(bf16)
 
     cc.wait_send()
     fc.wait_send()
+    zb.wait_send()
     drain(prs, s_prs)
     drain(lowf.at[pl.ds(0, 7)], s_pag)
-    drain(cgat, s_cot)
+    drain(cgat.at[0], s_gz)
+    drain(cgat.at[pl.ds(0, 6)], s_ag)
     drain(hrecv, s_dp)
     drain(fac.at[pl.ds(0, 15)], s_fac)
-    drain(yrecv, s_y)
+    drain(za, s_za)
+    for c in range(3):
+        for sem in (s_p1, s_raw, s_p2):
+            drain(far.at[c], sem.at[c])
     drain(lrecv, s_low)
+
+
+def hand_over(*refs):
+    n = len(refs) // 2
+    for i in range(n):
+        refs[n + i][...] = refs[i][...]
 
 
 def per_device(
@@ -326,7 +457,7 @@
     dma = pltpu.SemaphoreType.DMA
     V = pltpu.VMEM
     shp = jax.ShapeDtypeStruct
-    return pl.pallas_call(
+    results = pl.pallas_call(
         kernel,
         out_shape=(
             shp((256, 512), bf16), shp((4, 4, 64), f32), shp((2, 640), f32), shp((4, 4, 64), f32),
@@ -338,17 +469,18 @@
             V((256, 512), bf16), V((256, 640), bf16), V((8, 512, 640), bf16), V((4, 64, 128), bf16),
             V((64, 640), bf16), V((128, 48, 128), bf16), V((128, 48, 128), bf16), V((3, 128, 512), bf16),
             V((3, 128, 128), bf16), V((3, 128, 128), bf16),
-            V((512, 512), bf16), V((512, 320), bf16), V((320, 512), bf16), V((384, 384), bf16),
+            V((512, 512), bf16), V((512, 320), bf16), V((320, 512), bf16), V((192, 192), bf16),
             V((16, 768), jnp.int32), V((192, 48), f32), V((128, 128), f32),
             V((8, 32, 128), f32), V((7, 32, 128), f32), V((32, 128), bf16), V((8, 32, 128), bf16),
-            V((7, 256, 640), bf16), V((256, 512), f32),
+            V((8, 256, 640), bf16), V((256, 512), f32),
             V((32, 32, 128), bf16), V((16, 32, 128), bf16), V((16, 32, 128), bf16), V((15, 32, 128), bf16),
             V((16, 128), f32), V((16, 128), f32), V((32, 32, 128), bf16),
             V((3, 128, 512), bf16), V((384, 512), bf16), V((384, 512), bf16),
-            V((7, 384, 640), bf16), V((384, 640), f32), V((7, 384, 640), bf16),
-            V((192, 128), bf16), V((7, 192, 128), bf16),
-            dma((17,)), dma, dma, dma, dma, dma, dma((7,)), dma, dma, dma, dma,
-            dma, dma, dma, dma, dma, dma((7,)), dma, dma,
+            V((8, 384, 640), bf16), V((384, 640), f32), V((4, 192, 640), bf16),
+            V((3, 2, 96, 640), bf16), V((3, 2, 2, 96, 640), bf16), V((192, 640), bf16), V((192, 128), bf16), V((7, 192, 128), bf16),
+            dma((17,)), dma, dma, dma, dma, dma, dma((2, 6)), dma, dma((2,)), dma, dma, dma, dma,
+            dma, dma, dma, dma, dma, dma((4,)), dma((3,)), dma((3, 2)), dma((3,)), dma((3, 2)), dma((3,)), dma((3, 2)),
+            dma, dma, dma, dma,
         ],
         compiler_params=pltpu.CompilerParams(
             collective_id=0, has_side_effects=True, vmem_limit_bytes=56 << 20
@@ -361,6 +493,14 @@
         key_cache.reshape(128, 48, 128), value_cache.reshape(128, 48, 128), lengths.reshape(1, 128),
         new_query.swapaxes(0, 1), new_key.swapaxes(0, 1), new_value.swapaxes(0, 1),
     )
+    return pl.pallas_call(
+        hand_over,
+        out_shape=tuple(shp(r.shape, r.dtype) for r in results),
+        in_specs=[vmem] * 8,
+        out_specs=(vmem,) * 8,
+        cost_estimate=pl.CostEstimate(flops=0, bytes_accessed=2 << 20, transcendentals=0),
+        name="hand_over",
+    )(*results)
 
 
 def solution(mesh):

time: 143 us -> 70.5 us (0.49)
  Pallas kernels: 130 us -> 69.7 us
  local copies, waits for them, and re-layouts: 11.3 us -> 0 us
    pallas_call x1, Pallas kernels: 130 us -> 67.6 us  [per_device(): pl.pallas_call(kernel, out_shape=(shp((256, 512), bf16), shp((4, 4, 64),...]
    unnamed x8 -> x0, local copies, waits for them, and re-layouts: 11.3 us -> none
    pallas_call x0 -> x1, Pallas kernels: none -> 2.12 us  [per_device(): pl.pallas_call(hand_over, out_shape=tuple((shp(r.shape, r.dtype) for r in...]
where the time goes in v2:
time: 70.5 us; the launch traced here: 70.3 us
  Pallas kernels  69.7 us (99%)
    pallas_call x1, Pallas kernels, per_device(): pl.pallas_call(kernel, out_shape=(shp((256, 512), bf16), shp((4, 4, 64),...  67.6 us
    pallas_call x1, Pallas kernels, per_device(): pl.pallas_call(hand_over, out_shape=tuple((shp(r.shape, r.dtype) for r in...  2.12 us

profile of v2, /device:TPU:1, one launch (start us, length us, event | category | flops | bytes accessed | tf_op | source)
XLA Modules:
  0.0 70.3 jit_solution(3956829340535855946)
XLA Ops:
  0.6 67.6 %update_and_decode.1 = (bf16[256,512]{1,0:T(8,128)(2,1)}, f32[4,4,64]{2,1,0:T(4,128)}, f32[2,640]{1,0:T(2,128)}, f32[4,4,64]{2,1,0:T(4,128)}, f32[2,640]{1,0:T(2...) custom-call(bf16[256,512]{1,0:T(8,128)(2,1)} %acts_h.1, bf16[256,640]{1,0:T(8,128)(2,1)} %cot_h.1, ...), custom_call_target="tpu_custom_call" | custom-call | flops 4294967296 | bytes 12582912 | tf_op jit(solution)/shard_map/update_and_decode/pallas_call | solution.py:460
  68.2 2.1 %hand_over.1 = (bf16[256,512]{1,0:T(8,128)(2,1)}, f32[4,4,64]{2,1,0:T(4,128)}, f32[2,640]{1,0:T(2,128)}, f32[4,4,64]{2,1,0:T(4,128)}, f32[2,640]{1,0:T(2,128)}, ...) custom-call(bf16[256,512]{1,0:T(8,128)(2,1)} %get-tuple-element.16.refs_0_, ...), custom_call_target="tpu_custom_call" | custom-call | bytes 2097152 | tf_op jit(solution)/shard_map/hand_over/pallas_call | solution.py:496

commit v3 on v2

--- a/solution.py
+++ b/solution.py
@@ -42,16 +42,17 @@
 
 def kernel(
     acts_h, cot_h, w_h, olda_h, oldb_h,
-    ma, mb, oa, ob, va, vb,
-    key_h, val_h, len_ref, q_h, nk_h, nv_h,
+    ma_h, mb_h, oa_h, ob_h, va_h, vb_h,
+    key_h, val_h, len_h, q_h, nk_h, nv_h,
     grad_o, nma_o, nmb_o, noa_o, nob_o, nva_o, nvb_o, out_o,
     acts, cot, w, olda, oldb, keys, vals, q, nk, nv,
+    ma, mb, oa, ob, va, vb, len_ref,
     perma, spread, gather, permr, slotm, freshb, lencol,
     part, prs, lows, lowf, cgat, gacc,
-    gst, gpeer, hsum, hrecv, ga_s, gb_s, fac,
-    att, attp, att2, yb, yown, za, far, fin, zbr, lsend, lrecv,
-    lsem, s_prs, r_prs, s_pag, r_pag, s_ag, r_ag, s_gz, r_gz, s_core, r_core, s_dp, r_dp,
-    s_fac, r_fac, s_fcore, r_fcore, s_za, r_za, s_p1, r_p1, s_raw, r_raw, s_p2, r_p2, s_zb, r_zb, s_low, r_low,
+    gst, gpeer, hsum, xrecv, xsum, zrecv, ga_s, gb_s, fac,
+    att, attp, att2, yb, yown, za, far, fin, zbr, lsend, lpeer, lrecv,
+    lsem, s_prs, r_prs, s_pag, r_pag, s_ag, r_ag, s_gz, r_gz, s_gb, s_gbz, s_core, r_core, s_dx, r_dx, s_dz, r_dz,
+    s_fz, r_fz, s_fx, r_fx, s_fcore, r_fcore, s_za, r_za, s_p1, r_p1, s_raw, r_raw, s_p2, r_p2, s_zb, r_zb, s_lz, r_lz, s_low, r_low,
 ):
     dp = lax.axis_index("dp")
     t = lax.axis_index("tensor")
@@ -63,8 +64,13 @@
     def tpeer(k):
         return (dp, (t + k) % 8)
 
-    def cpeer(k):
-        return (((chip + k) % 16) * 2 + core, t)
+    cx, cz = chip // 4, chip % 4
+
+    def xpeer(k):
+        return ((((cx + k) % 4) * 4 + cz) * 2 + core, t)
+
+    def zpeer(k):
+        return ((cx * 4 + (cz + k) % 4) * 2 + core, t)
 
     corepeer = (chip * 2 + 1 - core, t)
     twin = (1 - z) * 4 + y
@@ -95,7 +101,9 @@
     ]
     for j in range(8):
         loads.append(pltpu.make_async_copy(w_h.at[:, pl.ds(j * 640, 640)], w.at[j], lsem.at[9 + j]))
-    for c in loads:
+    small = ((len_h, len_ref), (ma_h, ma), (mb_h, mb), (oa_h, oa), (ob_h, ob), (va_h, va), (vb_h, vb))
+    state = [pltpu.make_async_copy(a, b, lsem.at[17 + i]) for i, (a, b) in enumerate(small)]
+    for c in loads + state:
         c.start()
 
     bar = pltpu.get_barrier_semaphore()
@@ -105,11 +113,12 @@
         return 0
 
     def sig_c(k, _):
-        pl.semaphore_signal(bar, inc=1, device_id=cpeer(k), device_id_type=MESH)
+        pl.semaphore_signal(bar, inc=1, device_id=xpeer(k), device_id_type=MESH)
+        pl.semaphore_signal(bar, inc=1, device_id=zpeer(k), device_id_type=MESH)
         return 0
 
     lax.fori_loop(1, 8, sig_t, 0)
-    lax.fori_loop(1, 16, sig_c, 0)
+    lax.fori_loop(1, 4, sig_c, 0)
     pl.semaphore_signal(bar, inc=1, device_id=corepeer, device_id_type=MESH)
 
     for c in loads[:4]:
@@ -119,7 +128,7 @@
         low_p += mm(acts[:, h * 128 : (h + 1) * 128], olda[h], NT)
     thr_p = mm(cot[...], oldb[...], NT)
     part[...] = jnp.concatenate([low_p, thr_p], axis=1).reshape(8, 32, 128)
-    pl.semaphore_wait(bar, 23)
+    pl.semaphore_wait(bar, 14)
 
     def send_part(k, _):
         remote(part.at[(t + k) % 8], prs.at[7 - k], s_prs, r_prs, tpeer(k)).start()
@@ -127,27 +136,58 @@
 
     lax.fori_loop(1, 8, send_part, 0)
 
-    def half(h):
-        return pl.ds(h * 128, 128)
+    gather_b = pl.ds(0, 64)
+
+    def b_half(h):
+        return pl.ds(h * 32, 32)
+
+    def a_half(h):
+        return pl.ds(64 + h * 96, 96)
 
     def gather_own(h):
-        remote(cot.at[half(h)], cgat.at[t, half(h)], s_gz, r_gz.at[h], zdev).start()
-        for d in range(2):
-            remote(cot.at[half(h)], cgat.at[t, half(h)], s_ag, r_ag.at[d, h], ydev[d]).start()
+        remote(cot.at[a_half(h)], cgat.at[t, a_half(h)], s_gz, r_gz.at[h], zdev).start()
+        for d in range(2):
+            remote(cot.at[a_half(h)], cgat.at[t, a_half(h)], s_ag, r_ag.at[d, 1 + h], ydev[d]).start()
 
     def gather_twin(h):
-        drain(cgat.at[twin, half(h)], r_gz.at[h])
-        for d in range(2):
-            remote(cgat.at[twin, half(h)], cgat.at[twin, half(h)], s_ag, r_ag.at[d, 2 + h], ydev[d]).start()
+        blk = cgat.at[twin, a_half(h)]
+        drain(blk, r_gz.at[h])
+        for d in range(2):
+            remote(blk, blk, s_ag, r_ag.at[d, 3 + h], ydev[d]).start()
 
     def gather_relay(which):
         for d in range(2):
-            src = (z if which == 0 else 1 - z) * 4 + yprev[d]
-            blk = cgat.at[src, half(d)]
-            drain(blk, r_ag.at[d, which * 2 + d])
-            remote(blk, blk, s_ag, r_ag.at[d, 4 + which], ydev[d]).start()
-
+            blk = cgat.at[(z if which == 0 else 1 - z) * 4 + yprev[d], a_half(d)]
+            drain(blk, r_ag.at[d, 1 + which * 2 + d])
+            remote(blk, blk, s_ag, r_ag.at[d, 6 + which], ydev[d]).start()
+
+    def gather_b_own():
+        for d in range(2):
+            remote(cot.at[gather_b], cgat.at[t, gather_b], s_gb, r_ag.at[d, 0], ydev[d]).start()
+
+    def gather_b_relay():
+        for d in range(2):
+            drain(cgat.at[z * 4 + yprev[d], gather_b], r_ag.at[d, 0])
+            blk = cgat.at[z * 4 + yprev[d], b_half(d)]
+            remote(blk, blk, s_gb, r_ag.at[d, 5], ydev[d]).start()
+
+    def gather_b_twin():
+        remote(cot.at[gather_b], cgat.at[t, gather_b], s_gbz, r_gz.at[2], zdev).start()
+
+    def gather_b_next():
+        for d in range(2):
+            blk = cgat.at[z * 4 + yprev[d], gather_b]
+            remote(blk, blk, s_gbz, r_gz.at[3 + d], zdev).start()
+
+    def gather_b_far():
+        for d in range(2):
+            drain(cgat.at[z * 4 + yfar, b_half(d)], r_ag.at[d, 5])
+        blk = cgat.at[z * 4 + yfar, gather_b]
+        remote(blk, blk, s_gbz, r_gz.at[5], zdev).start()
+
+    gather_b_own()
     gather_own(0)
+    gather_b_twin()
 
     prow, pcol = iota((512, 512), 0), iota((512, 512), 1)
     blk = prow >> 4
@@ -172,6 +212,7 @@
     slotm[...] = jnp.where((slot >= 0) & (slot < 48), slot, 1000)
     fr, fc = iota((192, 48), 0), iota((192, 48), 1)
     freshb[...] = jnp.where(((fr & 15) == (fc & 15)) & ((fc >> 4) <= (fr >> 6)), 0.0, -1e30).astype(f32)
+    state[0].wait()
     diag = iota((128, 128), 0) == iota((128, 128), 1)
     lencol[...] = jnp.broadcast_to(
         jnp.sum(jnp.where(diag, len_ref[...].astype(f32), 0.0), axis=1, keepdims=True), (128, 128)
@@ -276,8 +317,9 @@
     for c in loads[9:]:
         c.wait()
     lax.fori_loop(other, other + 4, project(rows_a), 0)
-    send_za(0)
+    gather_b_relay()
     gather_twin(0)
+    gather_b_next()
     lax.fori_loop(4, 6, attend, 0)
 
     drain(lowf.at[pl.ds(0, 7)], r_pag)
@@ -295,32 +337,44 @@
     cc.start()
 
     lax.fori_loop(6, 8, attend, 0)
+    gather_twin(1)
+    gather_relay(0)
     cc.wait_recv()
     hsum[...] = (gst[pl.ds(core * 16, 16)].astype(f32) + gpeer[...].astype(f32)).astype(bf16)
 
-    def send_share(k, _):
-        remote(hsum.at[(chip + k) % 16], hrecv.at[15 - k], s_dp, r_dp, cpeer(k)).start()
-        return 0
-
-    lax.fori_loop(1, 16, send_share, 0)
-    gather_twin(1)
-    send_za(1)
+    for k in range(1, 4):
+        remote(hsum.at[pl.ds((cx + k) % 4 * 4, 4)], xrecv.at[3 - k], s_dx, r_dx, xpeer(k)).start()
+    send_za(yfar)
     order_rows(1)
     lax.fori_loop(other, other + 4, project(rows_b), 0)
+    y_far(2)
     lax.fori_loop(this, this + 4, project(rows_b), 0)
-    gather_relay(0)
-    y_far(2)
     y_far(1)
+    drain(xrecv, r_dx)
+    xtot = hsum[pl.ds(cx * 4, 4)].astype(f32)
+    for k in range(3):
+        xtot += xrecv[k].astype(f32)
+    xsum[...] = xtot.astype(bf16)
+    for k in range(1, 4):
+        remote(xsum.at[(cz + k) % 4], zrecv.at[3 - k], s_dz, r_dz, zpeer(k)).start()
     lax.fori_loop(this, this + 4, project(rows_a), 0)
     yown[...] = mm(attp[...], w[t])
     att2[...] = mm(attp[...], perma[...], NT).astype(bf16)
-
-    drain(hrecv, r_dp)
-
-    share = hsum[chip].astype(f32)
-    for k in range(15):
-        share += hrecv[k].astype(f32)
+    gather_b_far()
+
+    def add_za(j):
+        drain(za.at[j], r_za.at[j])
+        blk = yb.at[this + j, rows_a]
+        blk[...] = (blk[...].astype(f32) + za[j].astype(f32)).astype(bf16)
+
+    drain(zrecv, r_dz)
+
+    share = xsum[cz].astype(f32)
+    for k in range(3):
+        share += zrecv[k].astype(f32)
     share = share * (adapter_scale / 8192.0)
+    for c in state[1:]:
+        c.wait()
     gb_s[...] = share[0:16]
     ga_s[...] = share[16:32]
     for h in range(4):
@@ -337,26 +391,29 @@
     mine = core * 16 + chip
     fac[mine] = jnp.concatenate([gb_s[...], ga_s[...]], axis=0).astype(bf16)
 
-    def send_fac(k, _):
-        remote(fac.at[mine], fac.at[mine], s_fac, r_fac, cpeer(k)).start()
-        return 0
-
-    lax.fori_loop(1, 16, send_fac, 0)
-    send_za(2)
-    send_za(3)
+    for k in range(1, 4):
+        remote(fac.at[mine], fac.at[mine], s_fz, r_fz, zpeer(k)).start()
+    send_za(ynext[0])
+    send_za(ynext[1])
     gather_relay(1)
+    add_za(yfar)
+    y_far(0)
 
     thr = both[:, 64:128]
     add = [mm(thr, olda[h]) for h in range(4)]
     gacc[...] = adapter_scale * jnp.concatenate(add, axis=1) + mm(cot[...], w[t], NT)
-    gacc[...] += mm(cgat[twin], w[twin], NT)
 
     y_relay(2)
     y_raw(2)
+    mycol = pl.ds(core * 16 + cx * 4, 4)
+    drain(fac.at[pl.ds(0, 3)], r_fz)
+    for k in range(1, 4):
+        remote(fac.at[mycol], fac.at[mycol], s_fx, r_fx, xpeer(k)).start()
     y_relay(1)
+    y_raw(1)
 
     mycore = pl.ds(core * 16, 16)
-    drain(fac.at[pl.ds(0, 15)], r_fac)
+    drain(fac.at[pl.ds(0, 12)], r_fx)
     fc = remote(fac.at[mycore], fac.at[mycore], s_fcore, r_fcore, corepeer)
     fc.start()
     fc.wait_recv()
@@ -364,39 +421,22 @@
     a_new = fac[:, 16:32, :].reshape(512, 128)
     low = mm(att2[...], a_new)[:, 0:64]
     low = jnp.concatenate([low[0:192], low[192:384]], axis=1)
-    lsend[...] = low.astype(bf16)
-
-    def send_l(k, _):
-        remote(lsend, lrecv.at[7 - k], s_low, r_low, tpeer(k)).start()
-        return 0
-
-    lax.fori_loop(1, 8, send_l, 0)
+    lsend[0] = low.astype(bf16)
+    lz = remote(lsend.at[0], lpeer, s_lz, r_lz, zdev)
+    lz.start()
     b_new = mm(gather[...], fac[:, 0:16, :].reshape(512, 128)).astype(bf16)
     b_new = jnp.concatenate([b_new[c * 64 : (c + 1) * 64] for c in range(5)], axis=1)
 
-    for j in range(4):
-        drain(za.at[j], r_za.at[j])
-        blk = yb.at[this + j, rows_a]
-        blk[...] = (blk[...].astype(f32) + za[j].astype(f32)).astype(bf16)
-    yown[rows_a] += za[y].astype(f32)
-    y_far(0)
-    y_raw(1)
+    lz.wait_recv()
+    low += lpeer[...].astype(f32)
+    lsend[1] = low.astype(bf16)
+    for k in range(1, 4):
+        remote(lsend.at[1], lrecv.at[3 - k], s_low, r_low, (dp, this + (y + k) % 4)).start()
 
     for d in range(2):
-        for h in range(2):
-            if h != d:
-                drain(cgat.at[this + yprev[d], half(h)], r_ag.at[d, h])
-                drain(cgat.at[other + yprev[d], half(h)], r_ag.at[d, 2 + h])
-        drain(cgat.at[this + yfar, half(d)], r_ag.at[d, 4])
-        drain(cgat.at[other + yfar, half(d)], r_ag.at[d, 5])
-
-    def accumulate(k, _):
-        src = jnp.where(k < 3, z, 1 - z) * 4 + (y + 1 + k % 3) % 4
-        gacc[...] += mm(cgat[src], w[src], NT)
-        return 0
-
-    lax.fori_loop(0, 6, accumulate, 0)
-    grad_o[...] = gacc[...].astype(bf16)
+        add_za(ynext[d])
+    y_relay(0)
+    y_raw(0)
 
     y_wait(2)
     for h in range(2):
@@ -404,18 +444,34 @@
         blk[...] = (blk[...].astype(f32) + y_total(2, h)).astype(bf16)
     zb = remote(yb.at[twin, rows_b], zbr, s_zb, r_zb, zdev)
     zb.start()
-
-    y_relay(0)
-    y_raw(0)
+    send_za(y)
+
+    for d in range(2):
+        for p in range(2):
+            drain(cgat.at[(other if p else this) + yprev[d], a_half(1 - d)], r_ag.at[d, 1 + p * 2 + 1 - d])
+            drain(cgat.at[(other if p else this) + yfar, a_half(d)], r_ag.at[d, 6 + p])
+        drain(cgat.at[other + yprev[d], gather_b], r_gz.at[3 + d])
+    drain(cgat.at[twin, gather_b], r_gz.at[2])
+    drain(cgat.at[other + yfar, gather_b], r_gz.at[5])
+
+    def accumulate(k, _):
+        src = jnp.where(k < 3, z, 1 - z) * 4 + (y + 1 + k) % 4
+        gacc[...] += mm(cgat[src], w[src], NT)
+        return 0
+
+    lax.fori_loop(0, 7, accumulate, 0)
+    grad_o[...] = gacc[...].astype(bf16)
 
     drain(lrecv, r_low)
-    for k in range(7):
+    for k in range(3):
         low += lrecv[k].astype(f32)
     low = jnp.concatenate([low[:, 0:64], low[:, 64:128]], axis=0)
     hi = low.astype(bf16)
     lo = (low - hi.astype(f32)).astype(bf16)
     yown[...] += adapter_scale * (mm(hi, b_new) + mm(lo, b_new))
 
+    drain(za.at[y], r_za.at[y])
+    yown[rows_a] += za[y].astype(f32)
     y_wait(1)
     for h in range(2):
         yown[pl.ds(192 + h * half_rows, half_rows)] += y_total(1, h)
@@ -429,12 +485,17 @@
     cc.wait_send()
     fc.wait_send()
     zb.wait_send()
+    lz.wait_send()
     drain(prs, s_prs)
     drain(lowf.at[pl.ds(0, 7)], s_pag)
-    drain(cgat.at[0], s_gz)
-    drain(cgat.at[pl.ds(0, 6)], s_ag)
-    drain(hrecv, s_dp)
-    drain(fac.at[pl.ds(0, 15)], s_fac)
+    drain(cgat.at[0, pl.ds(64, 192)], s_gz)
+    drain(cgat.at[pl.ds(0, 6), pl.ds(64, 192)], s_ag)
+    drain(cgat.at[pl.ds(0, 3), gather_b], s_gb)
+    drain(cgat.at[pl.ds(0, 4), gather_b], s_gbz)
+    drain(xrecv, s_dx)
+    drain(zrecv, s_dz)
+    drain(fac.at[pl.ds(0, 3)], s_fz)
+    drain(fac.at[pl.ds(0, 12)], s_fx)
     drain(za, s_za)
     for c in range(3):
         for sem in (s_p1, s_raw, s_p2):
@@ -443,9 +504,12 @@
 
 
 def hand_over(*refs):
-    n = len(refs) // 2
-    for i in range(n):
-        refs[n + i][...] = refs[i][...]
+    n = (len(refs) - 1) // 2
+    copies = [pltpu.make_async_copy(refs[i], refs[n + i], refs[-1].at[i]) for i in range(n)]
+    for c in copies:
+        c.start()
+    for c in copies:
+        c.wait()
 
 
 def per_device(
@@ -460,27 +524,31 @@
     results = pl.pallas_call(
         kernel,
         out_shape=(
-            shp((256, 512), bf16), shp((4, 4, 64), f32), shp((2, 640), f32), shp((4, 4, 64), f32),
-            shp((2, 640), f32), shp((4, 4, 64), f32), shp((2, 640), f32), shp((640, 384), bf16),
+            V((256, 512), bf16), V((4, 4, 64), f32), V((2, 640), f32), V((4, 4, 64), f32),
+            V((2, 640), f32), V((4, 4, 64), f32), V((2, 640), f32), V((640, 384), bf16),
         ),
-        in_specs=[hbm] * 5 + [vmem] * 6 + [hbm] * 2 + [vmem] + [hbm] * 3,
+        in_specs=[hbm] * 17,
         out_specs=(vmem,) * 8,
         scratch_shapes=[
             V((256, 512), bf16), V((256, 640), bf16), V((8, 512, 640), bf16), V((4, 64, 128), bf16),
             V((64, 640), bf16), V((128, 48, 128), bf16), V((128, 48, 128), bf16), V((3, 128, 512), bf16),
             V((3, 128, 128), bf16), V((3, 128, 128), bf16),
+            V((4, 4, 64), f32), V((2, 640), f32), V((4, 4, 64), f32), V((2, 640), f32),
+            V((4, 4, 64), f32), V((2, 640), f32), V((1, 128), jnp.int32),
             V((512, 512), bf16), V((512, 320), bf16), V((320, 512), bf16), V((192, 192), bf16),
             V((16, 768), jnp.int32), V((192, 48), f32), V((128, 128), f32),
             V((8, 32, 128), f32), V((7, 32, 128), f32), V((32, 128), bf16), V((8, 32, 128), bf16),
             V((8, 256, 640), bf16), V((256, 512), f32),
-            V((32, 32, 128), bf16), V((16, 32, 128), bf16), V((16, 32, 128), bf16), V((15, 32, 128), bf16),
+            V((32, 32, 128), bf16), V((16, 32, 128), bf16), V((16, 32, 128), bf16), V((3, 4, 32, 128), bf16),
+            V((4, 32, 128), bf16), V((3, 32, 128), bf16),
             V((16, 128), f32), V((16, 128), f32), V((32, 32, 128), bf16),
             V((3, 128, 512), bf16), V((384, 512), bf16), V((384, 512), bf16),
             V((8, 384, 640), bf16), V((384, 640), f32), V((4, 192, 640), bf16),
-            V((3, 2, 96, 640), bf16), V((3, 2, 2, 96, 640), bf16), V((192, 640), bf16), V((192, 128), bf16), V((7, 192, 128), bf16),
-            dma((17,)), dma, dma, dma, dma, dma, dma((2, 6)), dma, dma((2,)), dma, dma, dma, dma,
+            V((3, 2, 96, 640), bf16), V((3, 2, 2, 96, 640), bf16), V((192, 640), bf16), V((2, 192, 128), bf16), V((192, 128), bf16),
+            V((3, 192, 128), bf16),
+            dma((24,)), dma, dma, dma, dma, dma, dma((2, 8)), dma, dma((6,)), dma, dma, dma, dma, dma, dma, dma, dma, dma, dma,
             dma, dma, dma, dma, dma, dma((4,)), dma((3,)), dma((3, 2)), dma((3,)), dma((3, 2)), dma((3,)), dma((3, 2)),
-            dma, dma, dma, dma,
+            dma, dma, dma, dma, dma, dma,
         ],
         compiler_params=pltpu.CompilerParams(
             collective_id=0, has_side_effects=True, vmem_limit_bytes=56 << 20
@@ -497,10 +565,11 @@
         hand_over,
         out_shape=tuple(shp(r.shape, r.dtype) for r in results),
         in_specs=[vmem] * 8,
-        out_specs=(vmem,) * 8,
+        out_specs=(hbm,) * 8,
+        scratch_shapes=[dma((8,))],
         cost_estimate=pl.CostEstimate(flops=0, bytes_accessed=2 << 20, transcendentals=0),
         name="hand_over",
-    )(*results)
+    )(*(pltpu.with_memory_space_constraint(r, pltpu.VMEM) for r in results))
 
 
 def solution(mesh):

time: 70.5 us -> 62.6 us (0.89)
  Pallas kernels: 69.7 us -> 61.9 us
    pallas_call x1, Pallas kernels: 67.6 us -> 60.9 us  [per_device(): pl.pallas_call(kernel, out_shape=(V((256, 512), bf16), V((4, 4, 64), f32)...]
    pallas_call x1, Pallas kernels: 2.12 us -> 0.96 us  [per_device(): pl.pallas_call(hand_over, out_shape=tuple((shp(r.shape, r.dtype) for r in...]
where the time goes in v3:
time: 62.6 us; the launch traced here: 62.5 us
  Pallas kernels  61.9 us (99%)
  between operations  0.65 us (1%)
    pallas_call x1, Pallas kernels, per_device(): pl.pallas_call(kernel, out_shape=(V((256, 512), bf16), V((4, 4, 64), f32)...  60.9 us

profile of v3, /device:TPU:1, one launch (start us, length us, event | category | flops | bytes accessed | tf_op | source)
XLA Modules:
  0.0 62.5 jit_solution(10150479819368358941)
XLA Ops:
  0.6 60.9 %update_and_decode.1 = (bf16[256,512]{1,0:T(8,128)(2,1)S(1)}, f32[4,4,64]{2,1,0:T(4,128)S(1)}, f32[2,640]{1,0:T(2,128)S(1)}, f32[4,4,64]{2,1,0:T(4,128)S(1)}, f3...) custom-call(bf16[256,512]{1,0:T(8,128)(2,1)} %acts_h.1, ...), custom_call_target="tpu_custom_call" | custom-call | flops 4294967296 | bytes 12582912 | tf_op jit(solution)/shard_map/update_and_decode/pallas_call | solution.py:524
  61.5 1.0 %hand_over.1 = (bf16[256,512]{1,0:T(8,128)(2,1)}, f32[4,4,64]{2,1,0:T(4,128)}, f32[2,640]{1,0:T(2,128)}, f32[4,4,64]{2,1,0:T(4,128)}, f32[2,640]{1,0:T(2,128)}, ...) custom-call(bf16[256,512]{1,0:T(8,128)(2,1)S(1)} %get-tuple-element.16.refs_0_, ...), custom_call_target="tpu_custom_call" | custom-call | bytes 2097152 | tf_op jit(solution)/shard_map/hand_over/pallas_call | solution.py:564

commit v4 on v3

--- a/solution.py
+++ b/solution.py
@@ -121,72 +121,77 @@
     lax.fori_loop(1, 4, sig_c, 0)
     pl.semaphore_signal(bar, inc=1, device_id=corepeer, device_id_type=MESH)
 
-    for c in loads[:4]:
+    pl.semaphore_wait(bar, 14)
+
+    gather_b = pl.ds(0, 96)
+
+    def b_half(h):
+        return pl.ds(h * 48, 48)
+
+    def a_half(h):
+        return pl.ds(96 + h * 80, 80)
+
+    def gather_own_z(h):
+        remote(cot.at[a_half(h)], cgat.at[t, a_half(h)], s_gz, r_gz.at[h], zdev).start()
+
+    def gather_own_y(h):
+        for d in range(2):
+            remote(cot.at[a_half(h)], cgat.at[t, a_half(h)], s_ag, r_ag.at[d, 1 + h], ydev[d]).start()
+
+    def gather_twin(h):
+        blk = cgat.at[twin, a_half(h)]
+        drain(blk, r_gz.at[h])
+        for d in range(2):
+            remote(blk, blk, s_ag, r_ag.at[d, 3 + h], ydev[d]).start()
+
+    def gather_relay(which):
+        for d in range(2):
+            blk = cgat.at[(z if which == 0 else 1 - z) * 4 + yprev[d], a_half(d)]
+            drain(blk, r_ag.at[d, 1 + which * 2 + d])
+            remote(blk, blk, s_ag, r_ag.at[d, 6 + which], ydev[d]).start()
+
+    def gather_b_own():
+        for d in range(2):
+            remote(cot.at[gather_b], cgat.at[t, gather_b], s_gb, r_ag.at[d, 0], ydev[d]).start()
+
+    def gather_b_relay():
+        for d in range(2):
+            drain(cgat.at[z * 4 + yprev[d], gather_b], r_ag.at[d, 0])
+            blk = cgat.at[z * 4 + yprev[d], b_half(d)]
+            remote(blk, blk, s_gb, r_ag.at[d, 5], ydev[d]).start()
+
+    def gather_b_twin():
+        remote(cot.at[gather_b], cgat.at[t, gather_b], s_gbz, r_gz.at[2], zdev).start()
+
+    def gather_b_next():
+        for d in range(2):
+            blk = cgat.at[z * 4 + yprev[d], gather_b]
+            remote(blk, blk, s_gbz, r_gz.at[3 + d], zdev).start()
+
+    def gather_b_far():
+        for d in range(2):
+            drain(cgat.at[z * 4 + yfar, b_half(d)], r_ag.at[d, 5])
+        blk = cgat.at[z * 4 + yfar, gather_b]
+        remote(blk, blk, s_gbz, r_gz.at[5], zdev).start()
+
+    loads[1].wait()
+    gather_b_own()
+    gather_own_z(0)
+
+    for c in (loads[0], loads[2], loads[3]):
         c.wait()
     low_p = mm(acts[:, 0:128], olda[0], NT)
     for h in range(1, 4):
         low_p += mm(acts[:, h * 128 : (h + 1) * 128], olda[h], NT)
     thr_p = mm(cot[...], oldb[...], NT)
-    part[...] = jnp.concatenate([low_p, thr_p], axis=1).reshape(8, 32, 128)
-    pl.semaphore_wait(bar, 14)
-
+    part[...] = jnp.concatenate([low_p, thr_p], axis=1).astype(bf16).reshape(8, 32, 128)
     def send_part(k, _):
         remote(part.at[(t + k) % 8], prs.at[7 - k], s_prs, r_prs, tpeer(k)).start()
         return 0
 
     lax.fori_loop(1, 8, send_part, 0)
 
-    gather_b = pl.ds(0, 64)
-
-    def b_half(h):
-        return pl.ds(h * 32, 32)
-
-    def a_half(h):
-        return pl.ds(64 + h * 96, 96)
-
-    def gather_own(h):
-        remote(cot.at[a_half(h)], cgat.at[t, a_half(h)], s_gz, r_gz.at[h], zdev).start()
-        for d in range(2):
-            remote(cot.at[a_half(h)], cgat.at[t, a_half(h)], s_ag, r_ag.at[d, 1 + h], ydev[d]).start()
-
-    def gather_twin(h):
-        blk = cgat.at[twin, a_half(h)]
-        drain(blk, r_gz.at[h])
-        for d in range(2):
-            remote(blk, blk, s_ag, r_ag.at[d, 3 + h], ydev[d]).start()
-
-    def gather_relay(which):
-        for d in range(2):
-            blk = cgat.at[(z if which == 0 else 1 - z) * 4 + yprev[d], a_half(d)]
-            drain(blk, r_ag.at[d, 1 + which * 2 + d])
-            remote(blk, blk, s_ag, r_ag.at[d, 6 + which], ydev[d]).start()
-
-    def gather_b_own():
-        for d in range(2):
-            remote(cot.at[gather_b], cgat.at[t, gather_b], s_gb, r_ag.at[d, 0], ydev[d]).start()
-
-    def gather_b_relay():
-        for d in range(2):
-            drain(cgat.at[z * 4 + yprev[d], gather_b], r_ag.at[d, 0])
-            blk = cgat.at[z * 4 + yprev[d], b_half(d)]
-            remote(blk, blk, s_gb, r_ag.at[d, 5], ydev[d]).start()
-
-    def gather_b_twin():
-        remote(cot.at[gather_b], cgat.at[t, gather_b], s_gbz, r_gz.at[2], zdev).start()
-
-    def gather_b_next():
-        for d in range(2):
-            blk = cgat.at[z * 4 + yprev[d], gather_b]
-            remote(blk, blk, s_gbz, r_gz.at[3 + d], zdev).start()
-
-    def gather_b_far():
-        for d in range(2):
-            drain(cgat.at[z * 4 + yfar, b_half(d)], r_ag.at[d, 5])
-        blk = cgat.at[z * 4 + yfar, gather_b]
-        remote(blk, blk, s_gbz, r_gz.at[5], zdev).start()
-
-    gather_b_own()
-    gather_own(0)
+    gather_own_y(0)
     gather_b_twin()
 
     prow, pcol = iota((512, 512), 0), iota((512, 512), 1)
@@ -261,8 +266,9 @@
 
     this, other = z * 4, (1 - z) * 4
 
-    def send_za(j):
-        remote(yb.at[other + j, rows_a], za.at[j], s_za, r_za.at[j], zdev).start()
+    def send_za(j, h):
+        part_h = pl.ds(h * 96, 96)
+        remote(yb.at[other + j, part_h], za.at[j, part_h], s_za, r_za.at[j], zdev).start()
 
     half_rows = 96
     classes = ((0, z), (192, z), (192, 1 - z))
@@ -301,10 +307,12 @@
     lax.fori_loop(0, 4, attend, 0)
     order_rows(0)
 
+    gather_own_z(1)
+    gather_own_y(1)
     drain(prs, r_prs)
-    tot = part[t]
+    tot = part[t].astype(f32)
     for k in range(7):
-        tot += prs[k]
+        tot += prs[k].astype(f32)
     lows[...] = tot.astype(bf16)
     lowf[t] = tot.astype(bf16)
 
@@ -313,7 +321,6 @@
         return 0
 
     lax.fori_loop(1, 8, send_low, 0)
-    gather_own(1)
     for c in loads[9:]:
         c.wait()
     lax.fori_loop(other, other + 4, project(rows_a), 0)
@@ -344,7 +351,8 @@
 
     for k in range(1, 4):
         remote(hsum.at[pl.ds((cx + k) % 4 * 4, 4)], xrecv.at[3 - k], s_dx, r_dx, xpeer(k)).start()
-    send_za(yfar)
+    send_za(yfar, 0)
+    send_za(yfar, 1)
     order_rows(1)
     lax.fori_loop(other, other + 4, project(rows_b), 0)
     y_far(2)
@@ -357,15 +365,21 @@
     xsum[...] = xtot.astype(bf16)
     for k in range(1, 4):
         remote(xsum.at[(cz + k) % 4], zrecv.at[3 - k], s_dz, r_dz, zpeer(k)).start()
+    gather_b_far()
     lax.fori_loop(this, this + 4, project(rows_a), 0)
     yown[...] = mm(attp[...], w[t])
     att2[...] = mm(attp[...], perma[...], NT).astype(bf16)
-    gather_b_far()
-
     def add_za(j):
         drain(za.at[j], r_za.at[j])
         blk = yb.at[this + j, rows_a]
         blk[...] = (blk[...].astype(f32) + za[j].astype(f32)).astype(bf16)
+
+    gather_relay(1)
+    add_za(yfar)
+    y_far(0)
+    y_raw(2)
+    y_raw(1)
+    send_za(ynext[0], 0)
 
     drain(zrecv, r_dz)
 
@@ -393,24 +407,22 @@
 
     for k in range(1, 4):
         remote(fac.at[mine], fac.at[mine], s_fz, r_fz, zpeer(k)).start()
-    send_za(ynext[0])
-    send_za(ynext[1])
-    gather_relay(1)
-    add_za(yfar)
-    y_far(0)
+    send_za(ynext[0], 1)
+    for h in range(2):
+        send_za(ynext[1], h)
+    for h in range(2):
+        send_za(y, h)
 
     thr = both[:, 64:128]
     add = [mm(thr, olda[h]) for h in range(4)]
     gacc[...] = adapter_scale * jnp.concatenate(add, axis=1) + mm(cot[...], w[t], NT)
 
     y_relay(2)
-    y_raw(2)
+    y_relay(1)
     mycol = pl.ds(core * 16 + cx * 4, 4)
     drain(fac.at[pl.ds(0, 3)], r_fz)
     for k in range(1, 4):
         remote(fac.at[mycol], fac.at[mycol], s_fx, r_fx, xpeer(k)).start()
-    y_relay(1)
-    y_raw(1)
 
     mycore = pl.ds(core * 16, 16)
     drain(fac.at[pl.ds(0, 12)], r_fx)
@@ -427,12 +439,6 @@
     b_new = mm(gather[...], fac[:, 0:16, :].reshape(512, 128)).astype(bf16)
     b_new = jnp.concatenate([b_new[c * 64 : (c + 1) * 64] for c in range(5)], axis=1)
 
-    lz.wait_recv()
-    low += lpeer[...].astype(f32)
-    lsend[1] = low.astype(bf16)
-    for k in range(1, 4):
-        remote(lsend.at[1], lrecv.at[3 - k], s_low, r_low, (dp, this + (y + k) % 4)).start()
-
     for d in range(2):
         add_za(ynext[d])
     y_relay(0)
@@ -444,7 +450,12 @@
         blk[...] = (blk[...].astype(f32) + y_total(2, h)).astype(bf16)
     zb = remote(yb.at[twin, rows_b], zbr, s_zb, r_zb, zdev)
     zb.start()
-    send_za(y)
+
+    lz.wait_recv()
+    low += lpeer[...].astype(f32)
+    lsend[1] = low.astype(bf16)
+    for k in range(1, 4):
+        remote(lsend.at[1], lrecv.at[3 - k], s_low, r_low, (dp, this + (y + k) % 4)).start()
 
     for d in range(2):
         for p in range(2):
@@ -488,8 +499,8 @@
     lz.wait_send()
     drain(prs, s_prs)
     drain(lowf.at[pl.ds(0, 7)], s_pag)
-    drain(cgat.at[0, pl.ds(64, 192)], s_gz)
-    drain(cgat.at[pl.ds(0, 6), pl.ds(64, 192)], s_ag)
+    drain(cgat.at[0, pl.ds(96, 160)], s_gz)
+    drain(cgat.at[pl.ds(0, 6), pl.ds(96, 160)], s_ag)
     drain(cgat.at[pl.ds(0, 3), gather_b], s_gb)
     drain(cgat.at[pl.ds(0, 4), gather_b], s_gbz)
     drain(xrecv, s_dx)
@@ -537,7 +548,7 @@
             V((4, 4, 64), f32), V((2, 640), f32), V((1, 128), jnp.int32),
             V((512, 512), bf16), V((512, 320), bf16), V((320, 512), bf16), V((192, 192), bf16),
             V((16, 768), jnp.int32), V((192, 48), f32), V((128, 128), f32),
-            V((8, 32, 128), f32), V((7, 32, 128), f32), V((32, 128), bf16), V((8, 32, 128), bf16),
+            V((8, 32, 128), bf16), V((7, 32, 128), bf16), V((32, 128), bf16), V((8, 32, 128), bf16),
             V((8, 256, 640), bf16), V((256, 512), f32),
             V((32, 32, 128), bf16), V((16, 32, 128), bf16), V((16, 32, 128), bf16), V((3, 4, 32, 128), bf16),
             V((4, 32, 128), bf16), V((3, 32, 128), bf16),

time: 62.6 us -> 59.6 us (0.952)
  Pallas kernels: 61.9 us -> 58.9 us
    pallas_call x1, Pallas kernels: 60.9 us -> 57.9 us  [per_device(): pl.pallas_call(kernel, out_shape=(V((256, 512), bf16), V((4, 4, 64), f32)...]
where the time goes in v4:
time: 59.6 us
  Pallas kernels  58.9 us (99%)
  between operations  0.65 us (1%)
    pallas_call x1, Pallas kernels, per_device(): pl.pallas_call(kernel, out_shape=(V((256, 512), bf16), V((4, 4, 64), f32)...  57.9 us

profile of v4, /device:TPU:1, one launch (start us, length us, event | category | flops | bytes accessed | tf_op | source)
XLA Modules:
  0.0 59.6 jit_solution(3934749398101029369)
XLA Ops:
  0.6 57.9 %update_and_decode.1 = (bf16[256,512]{1,0:T(8,128)(2,1)S(1)}, f32[4,4,64]{2,1,0:T(4,128)S(1)}, f32[2,640]{1,0:T(2,128)S(1)}, f32[4,4,64]{2,1,0:T(4,128)S(1)}, f3...) custom-call(bf16[256,512]{1,0:T(8,128)(2,1)} %acts_h.1, ...), custom_call_target="tpu_custom_call" | custom-call | flops 4294967296 | bytes 12582912 | tf_op jit(solution)/shard_map/update_and_decode/pallas_call | solution.py:535
  58.6 1.0 %hand_over.1 = (bf16[256,512]{1,0:T(8,128)(2,1)}, f32[4,4,64]{2,1,0:T(4,128)}, f32[2,640]{1,0:T(2,128)}, f32[4,4,64]{2,1,0:T(4,128)}, f32[2,640]{1,0:T(2,128)}, ...) custom-call(bf16[256,512]{1,0:T(8,128)(2,1)S(1)} %get-tuple-element.16.refs_0_, ...), custom_call_target="tpu_custom_call" | custom-call | bytes 2097152 | tf_op jit(solution)/shard_map/hand_over/pallas_call | solution.py:575

commit v5 on v4

--- a/solution.py
+++ b/solution.py
@@ -326,9 +326,12 @@
     lax.fori_loop(other, other + 4, project(rows_a), 0)
     gather_b_relay()
     gather_twin(0)
-    gather_b_next()
+    send_za(yfar, 0)
+    send_za(yfar, 1)
     lax.fori_loop(4, 6, attend, 0)
 
+    gather_twin(1)
+    gather_relay(0)
     drain(lowf.at[pl.ds(0, 7)], r_pag)
 
     both = lowf[...].reshape(256, 128)
@@ -342,17 +345,15 @@
     gst[:, 16:32, :] = jnp.concatenate([ga, jnp.zeros_like(ga)], axis=1).astype(bf16).reshape(32, 16, 128)
     cc = remote(gst.at[pl.ds((1 - core) * 16, 16)], gpeer, s_core, r_core, corepeer)
     cc.start()
+    send_za(ynext[0], 0)
 
     lax.fori_loop(6, 8, attend, 0)
-    gather_twin(1)
-    gather_relay(0)
     cc.wait_recv()
     hsum[...] = (gst[pl.ds(core * 16, 16)].astype(f32) + gpeer[...].astype(f32)).astype(bf16)
 
     for k in range(1, 4):
         remote(hsum.at[pl.ds((cx + k) % 4 * 4, 4)], xrecv.at[3 - k], s_dx, r_dx, xpeer(k)).start()
-    send_za(yfar, 0)
-    send_za(yfar, 1)
+    send_za(ynext[0], 1)
     order_rows(1)
     lax.fori_loop(other, other + 4, project(rows_b), 0)
     y_far(2)
@@ -365,7 +366,7 @@
     xsum[...] = xtot.astype(bf16)
     for k in range(1, 4):
         remote(xsum.at[(cz + k) % 4], zrecv.at[3 - k], s_dz, r_dz, zpeer(k)).start()
-    gather_b_far()
+    send_za(ynext[1], 0)
     lax.fori_loop(this, this + 4, project(rows_a), 0)
     yown[...] = mm(attp[...], w[t])
     att2[...] = mm(attp[...], perma[...], NT).astype(bf16)
@@ -379,7 +380,6 @@
     y_far(0)
     y_raw(2)
     y_raw(1)
-    send_za(ynext[0], 0)
 
     drain(zrecv, r_dz)
 
@@ -407,11 +407,10 @@
 
     for k in range(1, 4):
         remote(fac.at[mine], fac.at[mine], s_fz, r_fz, zpeer(k)).start()
-    send_za(ynext[0], 1)
-    for h in range(2):
-        send_za(ynext[1], h)
-    for h in range(2):
-        send_za(y, h)
+    send_za(ynext[1], 1)
+    gather_b_next()
+    gather_b_far()
+    send_za(y, 0)
 
     thr = both[:, 64:128]
     add = [mm(thr, olda[h]) for h in range(4)]
@@ -424,6 +423,11 @@
     for k in range(1, 4):
         remote(fac.at[mycol], fac.at[mycol], s_fx, r_fx, xpeer(k)).start()
 
+    for d in range(2):
+        add_za(ynext[d])
+    y_relay(0)
+    y_raw(0)
+
     mycore = pl.ds(core * 16, 16)
     drain(fac.at[pl.ds(0, 12)], r_fx)
     fc = remote(fac.at[mycore], fac.at[mycore], s_fcore, r_fcore, corepeer)
@@ -436,13 +440,15 @@
     lsend[0] = low.astype(bf16)
     lz = remote(lsend.at[0], lpeer, s_lz, r_lz, zdev)
     lz.start()
+    send_za(y, 1)
     b_new = mm(gather[...], fac[:, 0:16, :].reshape(512, 128)).astype(bf16)
     b_new = jnp.concatenate([b_new[c * 64 : (c + 1) * 64] for c in range(5)], axis=1)
 
-    for d in range(2):
-        add_za(ynext[d])
-    y_relay(0)
-    y_raw(0)
+    lz.wait_recv()
+    low += lpeer[...].astype(f32)
+    lsend[1] = low.astype(bf16)
+    for k in range(1, 4):
+        remote(lsend.at[1], lrecv.at[3 - k], s_low, r_low, (dp, this + (y + k) % 4)).start()
 
     y_wait(2)
     for h in range(2):
@@ -450,12 +456,6 @@
         blk[...] = (blk[...].astype(f32) + y_total(2, h)).astype(bf16)
     zb = remote(yb.at[twin, rows_b], zbr, s_zb, r_zb, zdev)
     zb.start()
-
-    lz.wait_recv()
-    low += lpeer[...].astype(f32)
-    lsend[1] = low.astype(bf16)
-    for k in range(1, 4):
-        remote(lsend.at[1], lrecv.at[3 - k], s_low, r_low, (dp, this + (y + k) % 4)).start()
 
     for d in range(2):
         for p in range(2):

time: 59.6 us -> 59.1 us (level)
  no operation moved by 1% of the time
where the time goes in v5:
time: 59.1 us; the launch traced here: 59 us
  Pallas kernels  58.4 us (99%)
  between operations  0.65 us (1%)
    pallas_call x1, Pallas kernels, per_device(): pl.pallas_call(kernel, out_shape=(V((256, 512), bf16), V((4, 4, 64), f32)...  57.4 us

profile of v5, /device:TPU:1, one launch (start us, length us, event | category | flops | bytes accessed | tf_op | source)
XLA Modules:
  0.0 59.0 jit_solution(17616016420321523157)
XLA Ops:
  0.6 57.4 %update_and_decode.1 = (bf16[256,512]{1,0:T(8,128)(2,1)S(1)}, f32[4,4,64]{2,1,0:T(4,128)S(1)}, f32[2,640]{1,0:T(2,128)S(1)}, f32[4,4,64]{2,1,0:T(4,128)S(1)}, f3...) custom-call(bf16[256,512]{1,0:T(8,128)(2,1)} %acts_h.1, ...), custom_call_target="tpu_custom_call" | custom-call | flops 4294967296 | bytes 12582912 | tf_op jit(solution)/shard_map/update_and_decode/pallas_call | solution.py:535
  58.1 1.0 %hand_over.1 = (bf16[256,512]{1,0:T(8,128)(2,1)}, f32[4,4,64]{2,1,0:T(4,128)}, f32[2,640]{1,0:T(2,128)}, f32[4,4,64]{2,1,0:T(4,128)}, f32[2,640]{1,0:T(2,128)}, ...) custom-call(bf16[256,512]{1,0:T(8,128)(2,1)S(1)} %get-tuple-element.16.refs_0_, ...), custom_call_target="tpu_custom_call" | custom-call | bytes 2097152 | tf_op jit(solution)/shard_map/hand_over/pallas_call | solution.py:575

commit v6 on v5

--- a/solution.py
+++ b/solution.py
@@ -410,7 +410,6 @@
     send_za(ynext[1], 1)
     gather_b_next()
     gather_b_far()
-    send_za(y, 0)
 
     thr = both[:, 64:128]
     add = [mm(thr, olda[h]) for h in range(4)]
@@ -426,7 +425,6 @@
     for d in range(2):
         add_za(ynext[d])
     y_relay(0)
-    y_raw(0)
 
     mycore = pl.ds(core * 16, 16)
     drain(fac.at[pl.ds(0, 12)], r_fx)
@@ -440,6 +438,7 @@
     lsend[0] = low.astype(bf16)
     lz = remote(lsend.at[0], lpeer, s_lz, r_lz, zdev)
     lz.start()
+    send_za(y, 0)
     send_za(y, 1)
     b_new = mm(gather[...], fac[:, 0:16, :].reshape(512, 128)).astype(bf16)
     b_new = jnp.concatenate([b_new[c * 64 : (c + 1) * 64] for c in range(5)], axis=1)
@@ -449,6 +448,7 @@
     lsend[1] = low.astype(bf16)
     for k in range(1, 4):
         remote(lsend.at[1], lrecv.at[3 - k], s_low, r_low, (dp, this + (y + k) % 4)).start()
+    y_raw(0)
 
     y_wait(2)
     for h in range(2):

time: 59.1 us -> 59.4 us (level)
  no operation moved by 1% of the time
where the time goes in v6:
time: 59.4 us; the launch traced here: 59.3 us
  Pallas kernels  58.7 us (99%)
  between operations  0.65 us (1%)
    pallas_call x1, Pallas kernels, per_device(): pl.pallas_call(kernel, out_shape=(V((256, 512), bf16), V((4, 4, 64), f32)...  57.7 us

profile of v6, /device:TPU:1, one launch (start us, length us, event | category | flops | bytes accessed | tf_op | source)
XLA Modules:
  0.0 59.3 jit_solution(2209883410717519505)
XLA Ops:
  0.6 57.7 %update_and_decode.1 = (bf16[256,512]{1,0:T(8,128)(2,1)S(1)}, f32[4,4,64]{2,1,0:T(4,128)S(1)}, f32[2,640]{1,0:T(2,128)S(1)}, f32[4,4,64]{2,1,0:T(4,128)S(1)}, f3...) custom-call(bf16[256,512]{1,0:T(8,128)(2,1)} %acts_h.1, ...), custom_call_target="tpu_custom_call" | custom-call | flops 4294967296 | bytes 12582912 | tf_op jit(solution)/shard_map/update_and_decode/pallas_call | solution.py:535
  58.3 1.0 %hand_over.1 = (bf16[256,512]{1,0:T(8,128)(2,1)}, f32[4,4,64]{2,1,0:T(4,128)}, f32[2,640]{1,0:T(2,128)}, f32[4,4,64]{2,1,0:T(4,128)}, f32[2,640]{1,0:T(2,128)}, ...) custom-call(bf16[256,512]{1,0:T(8,128)(2,1)S(1)} %get-tuple-element.16.refs_0_, ...), custom_call_target="tpu_custom_call" | custom-call | bytes 2097152 | tf_op jit(solution)/shard_map/hand_over/pallas_call | solution.py:575
